TPU v7x, 512 devices: a whole 4x4x16 slice. The times are simulated.
512 devices in a mesh: seg: 64 (over y, z_lo, core), sec: 8 (over x, z_hi).
Axes of the slice: x: 4, y: 4, z: 16 (z_hi: 2, z_lo: 8; z = z_hi * 8 + z_lo), core: 2. Of those that a mesh axis runs over, the one named last changes fastest.
Arguments:
- psi_start: bfloat16 [64, 8, 512, 512], P('seg', 'sec'), may hold values from -6 to 6
- left_site: bfloat16 [64, 8, 512, 512], P('seg', 'sec'), may hold values from -2 to 2
- left_terms: bfloat16 [64, 8, 3, 512, 512], P('seg', 'sec'), may hold values from -20 to 20
- right_terms: bfloat16 [64, 8, 2, 512, 512], P('seg', 'sec'), may hold values from -1 to 1
- start_cols: bfloat16 [8, 512, 256], P('sec'), may hold values from -6 to 6
- sector_table: int32 [8, 3], P('sec'), may hold values from 128 to 512, as said below
Outputs:
- truncated: bfloat16 [64, 8, 512, 512], P('seg', 'sec')
- density_back: bfloat16 [64, 8, 512, 512], P('seg', 'sec')
Inputs may be any that keep to these rules, and one draw needn't show every extreme that they name: `sector_table`: live rows and live columns lie between 256 and 512, kept ranks between 128 and 256; some sector has 512 live rows and columns and rank 256.
All inputs are finite; a program needn't handle non-finite values.
Results may differ from a plain program's by a relative error of at most 0.024.
Values may be sent and summed in bfloat16 or wider, within the bound.
A program may use at most 64 MiB of HBM per device.

v0:
```python
import math

import jax
import jax.numpy as jnp
from jax import lax
from jax.sharding import PartitionSpec as P

eps = 1e-06


def from_behind(block, axis, distance):
    devices = range(lax.axis_size(axis))
    route = [(i - distance, i) for i in devices if i - distance in devices]
    return lax.ppermute(block, axis, route)


def build_left(site, terms):
    part = jnp.einsum("kij,jl->kil", terms, site, preferred_element_type=jnp.float32).astype(
        jnp.bfloat16
    )
    return jnp.einsum("ji,kjl->kil", site, part, preferred_element_type=jnp.float32).astype(
        jnp.bfloat16
    )


def product(left, right):
    return jnp.dot(left, right, preferred_element_type=jnp.float32)


def hamil(vector, env, right, mask):
    below = from_behind(vector, "sec", 1)
    above = from_behind(vector, "sec", -1)
    lower = product(below, right[0]).astype(jnp.bfloat16)
    upper = product(above, right[1]).astype(jnp.bfloat16)
    total = product(env[0], vector) + product(env[1], lower) + product(env[2], upper)
    return total * mask


def per_device(psi_start, left_site, left_terms, right_terms, start_cols, sector_table):
    site = left_site[0, 0]
    terms = left_terms[0, 0]
    right = right_terms[0, 0]
    cols = start_cols[0]
    table = sector_table[0]
    width = site.shape[0]
    kept_cols = cols.shape[1]
    env = from_behind(build_left(site, terms), "seg", 1)
    index = jnp.arange(width, dtype=jnp.int32)
    mask = ((index[:, None] < table[0]) & (index[None, :] < table[1])).astype(jnp.float32)
    keep = (jnp.arange(kept_cols, dtype=jnp.int32) < table[2]).astype(jnp.float32)
    start = psi_start[0, 0].astype(jnp.float32) * mask
    start_sum = lax.psum(jnp.sum(start * start), "sec")
    first = (start / jnp.sqrt(start_sum + eps)).astype(jnp.bfloat16)
    firstf = first.astype(jnp.float32)
    image = hamil(first, env, right, mask)
    alpha = lax.psum(jnp.sum(firstf * image), "sec")
    resid = image - alpha * firstf
    resid_sq = lax.psum(jnp.sum(resid * resid), "sec")
    beta = jnp.sqrt(resid_sq + eps)
    second = (resid / beta).astype(jnp.bfloat16)
    secondf = second.astype(jnp.float32)
    second_image = hamil(second, env, right, mask)
    gamma = lax.psum(jnp.sum(secondf * second_image), "sec")
    lowest = 0.5 * (alpha + gamma) - jnp.sqrt(0.25 * (alpha - gamma) ** 2 + beta**2)
    united = (gamma - lowest) * firstf - beta * secondf
    united_sq = lax.psum(jnp.sum(united * united), "sec")
    factor = math.sqrt(lax.axis_size("sec") * width * width) / jnp.sqrt(united_sq + eps)
    ground = (united * factor).astype(jnp.bfloat16)
    ranged = (product(ground, cols) * keep[None, :]).astype(jnp.bfloat16)
    rangef = ranged.astype(jnp.float32)
    gram = product(ranged.T, ranged) + jnp.eye(kept_cols, dtype=jnp.float32) * (1.0 - keep)[None, :]
    factors = jnp.linalg.cholesky(gram)
    solved = jax.scipy.linalg.solve_triangular(factors, rangef.T, lower=True)
    basis = solved.T.astype(jnp.bfloat16)
    coeff = product(basis.T, ground).astype(jnp.bfloat16)
    kept = product(basis, coeff).astype(jnp.bfloat16)
    dens = (product(kept, kept.T) / width).astype(jnp.bfloat16)
    back = from_behind(dens, "seg", -1)
    return (kept[None, None], back[None, None])


def solution(mesh):
    placed = (
        P("seg", "sec", None, None),
        P("seg", "sec", None, None),
        P("seg", "sec", None, None, None),
        P("seg", "sec", None, None, None),
        P("sec", None, None),
        P("sec", None),
    )
    return jax.shard_map(
        per_device,
        mesh=mesh,
        in_specs=placed,
        out_specs=(P("seg", "sec", None, None), P("seg", "sec", None, None)),
        check_vma=False,
    )
```

profile of v0, /device:TPU:1, one launch (start us, length us, event | category | flops | bytes accessed | tf_op | source)
XLA Modules:
  0.0 508.7 jit_solution(5524498703188277331)
XLA Ops:
  2.0 4.2 fusion.1
  6.2 4.9 collective-permute-start
  14.1 46.3 %psum.35 = f32[]{:T(128)} all-reduce(f32[]{:T(128)} %fusion.17), channel_id=1, replica_groups=mesh['seg'=64,'sec'=8] {'sec'}, use_global_device_ids=true, to_apply=%region_1.0 | all-reduce | flops 1 | bytes 8 | tf_op jit(solution)/shard_map/psum | solution.py:52
  61.4 13.1 %collective-permute-start.1 = (bf16[512,512]{1,0:T(8,128)(2,1)S(1)}, bf16[512,512]{1,0:T(8,128)(2,1)}, u32[]{:S(2)}, u32[]{:S(2)}) collective-permute-start(bf16[512,512]{1,0:T(8,128)(2,1)S(1)} %fusion.18), channel_id=1, source_target_pairs={{0,1},{1,2},{2,3},{3,4},{4,5},{5,6},{6,7},{8,9},{9,10},{10,11},{11... | collective-permute-start | bytes 1572872 | tf_op jit(solution)/shard_map/ppermute | solution.py:14
  75.8 13.6 %collective-permute-done.1 = bf16[512,512]{1,0:T(8,128)(2,1)} collective-permute-done((bf16[512,512]{1,0:T(8,128)(2,1)S(1)}, bf16[512,512]{1,0:T(8,128)(2,1)}, u32[]{:S(2)}, u32[]{:S(2)}) %collective-permute-start.1) | collective-permute-done | bytes 524320 | tf_op jit(solution)/shard_map/ppermute | solution.py:14
  89.4 3.1 fusion.6
  92.5 37.5 %collective-permute-done.2 = bf16[512,512]{1,0:T(8,128)(2,1)S(1)} collective-permute-done((bf16[512,512]{1,0:T(8,128)(2,1)S(1)}, bf16[512,512]{1,0:T(8,128)(2,1)S(1)}, u32[]{:S(2)}, u32[]{:S(2)}) %collective-permute-start.2) | collective-permute-done | bytes 524320 | tf_op jit(solution)/shard_map/ppermute | solution.py:14
  133.0 3.3 fusion.20
  136.3 43.8 %psum.36 = f32[]{:T(128)} all-reduce(f32[]{:T(128)} %get-tuple-element.27), channel_id=1, replica_groups=mesh['seg'=64,'sec'=8] {'sec'}, use_global_device_ids=true, to_apply=%region_3.0 | all-reduce | flops 1 | bytes 8 | tf_op jit(solution)/shard_map/psum | solution.py:56
  181.9 37.6 %psum.37 = f32[]{:T(128)} all-reduce(f32[]{:T(128)} %multiply_reduce_fusion.1), channel_id=1, replica_groups=mesh['seg'=64,'sec'=8] {'sec'}, use_global_device_ids=true, to_apply=%region_5.0 | all-reduce | flops 1 | bytes 8 | tf_op jit(solution)/shard_map/psum | solution.py:58
  222.0 6.0 %collective-permute-start.3 = (bf16[512,512]{1,0:T(8,128)(2,1)}, bf16[512,512]{1,0:T(8,128)(2,1)}, u32[]{:S(2)}, u32[]{:S(2)}) collective-permute-start(bf16[512,512]{1,0:T(8,128)(2,1)} %divide_convert_fusion), channel_id=1, source_target_pairs={{0,1},{1,2},{2,3},{3,4},{4,5},{5,6},{6,7},{8,9},{9,10},{10,11},{11... | collective-permute-start | bytes 1572872 | tf_op jit(solution)/shard_map/ppermute | solution.py:14
  230.6 3.3 collective-permute-done.3
  233.8 3.1 fusion.8
  236.9 19.7 %collective-permute-done.4 = bf16[512,512]{1,0:T(8,128)(2,1)} collective-permute-done((bf16[512,512]{1,0:T(8,128)(2,1)}, bf16[512,512]{1,0:T(8,128)(2,1)}, u32[]{:S(2)}, u32[]{:S(2)}) %collective-permute-start.4) | collective-permute-done | bytes 524320 | tf_op jit(solution)/shard_map/ppermute | solution.py:14
  259.6 3.3 fusion.22
  262.9 74.8 %psum.38 = f32[]{:T(128)} all-reduce(f32[]{:T(128)} %fusion.22), channel_id=1, replica_groups=mesh['seg'=64,'sec'=8] {'sec'}, use_global_device_ids=true, to_apply=%region_7.0 | all-reduce | flops 1 | bytes 8 | tf_op jit(solution)/shard_map/psum | solution.py:63
  342.9 41.2 %psum.39 = f32[]{:T(128)} all-reduce(f32[]{:T(128)} %multiply_reduce_fusion), channel_id=1, replica_groups=mesh['seg'=64,'sec'=8] {'sec'}, use_global_device_ids=true, to_apply=%region_9.0 | all-reduce | flops 1 | bytes 8 | tf_op jit(solution)/shard_map/psum | solution.py:66
  386.7 11.7 %cholesky.49 = f32[128,128]{1,0:T(8,128)S(1)} custom-call(f32[128,128]{1,0:T(8,128)S(1)} %cholesky.115), custom_call_target="Cholesky" | custom-call | tf_op jit(solution)/shard_map/jit(cholesky)/cholesky | solution.py:72
  398.5 9.8 %custom-call.15 = f32[1,128,128]{1,2,0:T(8,128)S(1)} custom-call(f32[1,128,128]{2,1,0:T(8,128)S(1)} %get-tuple-element.23), custom_call_target="InvertDiagBlocksLowerTriangular" | custom-call | tf_op jit(solution)/shard_map/jit(cholesky)/cholesky | solution.py:72
  408.8 11.7 %cholesky.103 = f32[128,128]{1,0:T(8,128)S(1)} custom-call(f32[128,128]{1,0:T(8,128)S(1)} %convolution_subtract_fusion.1), custom_call_target="Cholesky" | custom-call | tf_op jit(solution)/shard_map/jit(cholesky)/cholesky | solution.py:72
  423.1 3.8 while.1
  426.9 19.9 %custom-call.16 = f32[2,128,128]{1,2,0:T(8,128)S(1)} custom-call(f32[2,128,128]{2,1,0:T(8,128)S(1)} %get-tuple-element.9), custom_call_target="InvertDiagBlocksLowerTriangular" | custom-call | tf_op jit(solution)/shard_map/jit(_solve_triangular)/triangular_solve | solution.py:73
  450.4 18.9 %collective-permute-start.5 = (bf16[512,512]{1,0:T(8,128)(2,1)S(1)}, bf16[512,512]{1,0:T(8,128)(2,1)S(1)}, u32[]{:S(2)}, u32[]{:S(2)}) collective-permute-start(bf16[512,512]{1,0:T(8,128)(2,1)S(1)} %fusion.5), channel_id=1, source_target_pairs={{8,0},{16,8},{24,16},{32,24},{40,32},{48,40},{56,48},{64,56},{72,6... | collective-permute-start | bytes 1572872 | tf_op jit(solution)/shard_map/ppermute | solution.py:14
  469.3 38.6 %collective-permute-done.5 = bf16[512,512]{1,0:T(8,128)(2,1)S(1)} collective-permute-done((bf16[512,512]{1,0:T(8,128)(2,1)S(1)}, bf16[512,512]{1,0:T(8,128)(2,1)S(1)}, u32[]{:S(2)}, u32[]{:S(2)}) %collective-permute-start.5) | collective-permute-done | bytes 524320 | tf_op jit(solution)/shard_map/ppermute | solution.py:14
  (58 shorter events, 32.1 us)
Async XLA Ops:
  0.6 1.4 copy-start
  0.6 10.5 %copy-start.4 = (s32[1,3]{1,0:T(1,128)S(1)}, s32[1,3]{1,0:T(1,128)}, u32[]{:S(2)}) copy-start(s32[1,3]{1,0:T(1,128)} %param.11) | copy-start | bytes 40
  0.7 12.4 %copy-start.1 = (bf16[1,1,512,512]{3,2,1,0:T(8,128)(2,1)S(1)}, bf16[1,1,512,512]{3,2,1,0:T(8,128)(2,1)}, u32[]{:S(2)}) copy-start(bf16[1,1,512,512]{3,2,1,0:T(8,128)(2,1)} %param.6) | copy-start | bytes 1572868
  6.2 83.2 %collective-permute-start = (bf16[3,512,512]{1,2,0:T(8,128)(2,1)}, bf16[3,512,512]{1,2,0:T(8,128)(2,1)}, u32[]{:S(2)}, u32[]{:S(2)}) collective-permute-start(bf16[3,512,512]{1,2,0:T(8,128)(2,1)} %fusion.1), channel_id=1, source_target_pairs={{0,8},{8,16},{16,24},{24,32},{32,40},{40,48},{48,56},{56,64},{64,7... | collective-permute-start | bytes 4718600 | tf_op jit(solution)/shard_map/ppermute | solution.py:14
  61.4 31.1 %copy-start.2 = (bf16[512,512]{1,0:T(8,128)(2,1)}, bf16[512,512]{1,0:T(8,128)(2,1)S(1)}, u32[]{:S(2)}) copy-start(bf16[512,512]{1,0:T(8,128)(2,1)S(1)} %fusion.18) | copy-start | bytes 1572868
  61.4 28.0 %collective-permute-start.1 = (bf16[512,512]{1,0:T(8,128)(2,1)S(1)}, bf16[512,512]{1,0:T(8,128)(2,1)}, u32[]{:S(2)}, u32[]{:S(2)}) collective-permute-start(bf16[512,512]{1,0:T(8,128)(2,1)S(1)} %fusion.18), channel_id=1, source_target_pairs={{0,1},{1,2},{2,3},{3,4},{4,5},{5,6},{6,7},{8,9},{9,10},{10,11},{11... | collective-permute-start | bytes 1572872 | tf_op jit(solution)/shard_map/ppermute | solution.py:14
  74.5 55.5 %collective-permute-start.2 = (bf16[512,512]{1,0:T(8,128)(2,1)S(1)}, bf16[512,512]{1,0:T(8,128)(2,1)S(1)}, u32[]{:S(2)}, u32[]{:S(2)}) collective-permute-start(bf16[512,512]{1,0:T(8,128)(2,1)S(1)} %fusion.18), channel_id=1, source_target_pairs={{1,0},{2,1},{3,2},{4,3},{5,4},{6,5},{7,6},{9,8},{10,9},{11,10},{12... | collective-permute-start | bytes 1572872 | tf_op jit(solution)/shard_map/ppermute | solution.py:14
  222.0 11.8 %collective-permute-start.3 = (bf16[512,512]{1,0:T(8,128)(2,1)}, bf16[512,512]{1,0:T(8,128)(2,1)}, u32[]{:S(2)}, u32[]{:S(2)}) collective-permute-start(bf16[512,512]{1,0:T(8,128)(2,1)} %divide_convert_fusion), channel_id=1, source_target_pairs={{0,1},{1,2},{2,3},{3,4},{4,5},{5,6},{6,7},{8,9},{9,10},{10,11},{11... | collective-permute-start | bytes 1572872 | tf_op jit(solution)/shard_map/ppermute | solution.py:14
  228.0 28.6 %collective-permute-start.4 = (bf16[512,512]{1,0:T(8,128)(2,1)}, bf16[512,512]{1,0:T(8,128)(2,1)}, u32[]{:S(2)}, u32[]{:S(2)}) collective-permute-start(bf16[512,512]{1,0:T(8,128)(2,1)} %divide_convert_fusion), channel_id=1, source_target_pairs={{1,0},{2,1},{3,2},{4,3},{5,4},{6,5},{7,6},{9,8},{10,9},{11,10},{12... | collective-permute-start | bytes 1572872 | tf_op jit(solution)/shard_map/ppermute | solution.py:14
  230.5 26.1 %copy-start.5 = (bf16[1,1,2,512,512]{4,3,2,1,0:T(8,128)(2,1)S(1)}, bf16[1,1,2,512,512]{4,3,2,1,0:T(8,128)(2,1)}, u32[]{:S(2)}) copy-start(bf16[1,1,2,512,512]{4,3,2,1,0:T(8,128)(2,1)} %param.9) | copy-start | bytes 3145732
  259.6 125.1 %copy-start.3 = (bf16[512,512]{1,0:T(8,128)(2,1)S(1)}, bf16[512,512]{1,0:T(8,128)(2,1)}, u32[]{:S(2)}) copy-start(bf16[512,512]{1,0:T(8,128)(2,1)} %copy-done.2) | copy-start | bytes 1572868
  259.6 125.1 %copy-start.6 = (bf16[1,512,256]{2,1,0:T(8,128)(2,1)S(1)}, bf16[1,512,256]{2,1,0:T(8,128)(2,1)}, u32[]{:S(2)}) copy-start(bf16[1,512,256]{2,1,0:T(8,128)(2,1)} %param.10) | copy-start | bytes 786436
  449.9 58.8 %copy-start.7 = (bf16[512,512]{1,0:T(8,128)(2,1)}, bf16[512,512]{1,0:T(8,128)(2,1)S(1)}, u32[]{:S(2)}) copy-start(bf16[512,512]{1,0:T(8,128)(2,1)S(1)} %convolution_convert_fusion.6) | copy-start | bytes 1572868
  450.4 57.5 %collective-permute-start.5 = (bf16[512,512]{1,0:T(8,128)(2,1)S(1)}, bf16[512,512]{1,0:T(8,128)(2,1)S(1)}, u32[]{:S(2)}, u32[]{:S(2)}) collective-permute-start(bf16[512,512]{1,0:T(8,128)(2,1)S(1)} %fusion.5), channel_id=1, source_target_pairs={{8,0},{16,8},{24,16},{32,24},{40,32},{48,40},{56,48},{64,56},{72,6... | collective-permute-start | bytes 1572872 | tf_op jit(solution)/shard_map/ppermute | solution.py:14
where the time goes:
time: 510 us; the launch traced here: 509 us
  blocking collectives  244 us (48%)
  waiting for transfers between devices  113 us (22%)
  other arithmetic  64.2 us (13%)
  starting transfers between devices  45.5 us (9%)
  matrix products  28.7 us (6%)
  between operations  7.08 us (1%)
  local copies, waits for them, and re-layouts  6.83 us (1%)
    ppermute x6, waiting for transfers between devices, from_behind(): return lax.ppermute(block, axis, route)  113 us
    psum x1, blocking collectives, per_device(): gamma = lax.psum(jnp.sum(secondf * second_image), 'sec')  74.8 us
    psum x1, blocking collectives, per_device(): start_sum = lax.psum(jnp.sum(start * start), 'sec')  46.3 us
    ppermute x6, starting transfers between devices, from_behind(): return lax.ppermute(block, axis, route)  45.5 us
    psum x1, blocking collectives, per_device(): alpha = lax.psum(jnp.sum(firstf * image), 'sec')  43.8 us
    psum x1, blocking collectives, per_device(): united_sq = lax.psum(jnp.sum(united * united), 'sec')  41.2 us
    psum x1, blocking collectives, per_device(): resid_sq = lax.psum(jnp.sum(resid * resid), 'sec')  37.6 us
    another operation x7, other arithmetic, per_device(): factors = jnp.linalg.cholesky(gram)  34.6 us
  transfers between devices with their start and end apart: 6, of which 5 were waited for; matrix products, arithmetic and copies ran while one was open for 2% of the time, Pallas kernels for 0%

commit v1 on v0

v1 whole, which is shorter than its diff:
```python
import functools
import math

import jax
import jax.numpy as jnp
from jax import lax
from jax.experimental import pallas as pl
from jax.experimental.pallas import tpu as pltpu
from jax.sharding import PartitionSpec as P

eps = 1e-06
MESH = pl.DeviceIdType.MESH
CHUNKS = 8


def dot(left, right):
    return jnp.dot(left, right, preferred_element_type=jnp.float32)


def dot_t(left, right):
    return lax.dot_general(
        left, right, (((0,), (0,)), ((), ())), preferred_element_type=jnp.float32
    )


def total(block):
    return jnp.sum(jnp.sum(block, axis=0, keepdims=True), axis=1, keepdims=True)


def pack(values):
    row = lax.broadcasted_iota(jnp.int32, (8, 128), 0)
    tile = jnp.zeros((8, 128), jnp.float32)
    for k, value in enumerate(values):
        tile = jnp.where(row == k, value, tile)
    return tile


def lanczos_kernel(
    table_ref, psi_ref, site_ref, terms_ref, right_ref, ground_ref,
    start, start_z, start_x, site_t, part, built, env, vec, vec_z, vec_x,
    low_z, low_x, image, resid, resid_z, resid_x, adj_z, adj_x,
    sums1, sums2, sums3,
    z_send, z_recv, x_send, x_recv, env_send, env_recv, sum_send, sum_recv,
):
    seg, sec = lax.axis_index("seg"), lax.axis_index("sec")
    segs, secs = lax.axis_size("seg"), lax.axis_size("sec")
    width = psi_ref.shape[0]
    rows = width // CHUNKS
    half = width // 2
    parity = lax.rem(sec, 2)
    partner = sec + 1 - 2 * parity
    relay = lax.rem(sec + 2 - 4 * parity + secs, secs)
    origin = lax.rem(sec + 2 * parity - 1 + secs, secs)
    nxt, prv = lax.rem(seg + 1, segs), lax.rem(seg + segs - 1, segs)
    peers = [(seg, lax.rem(sec + d, secs)) for d in range(1, secs)]

    barrier = pltpu.get_barrier_semaphore()
    neighbours = peers + [(nxt, sec), (prv, sec)]
    for device in neighbours:
        pl.semaphore_signal(barrier, inc=1, device_id=device, device_id_type=MESH)
    pl.semaphore_wait(barrier, len(neighbours))

    def chunk(i):
        return pl.ds(pl.multiple_of(i * rows, rows), rows)

    def z_copy(phase, i, source, target):
        return pltpu.make_async_remote_copy(
            source.at[chunk(i)], target.at[chunk(i)],
            z_send.at[phase, i], z_recv.at[phase, i],
            device_id=(seg, partner), device_id_type=MESH,
        )

    def x_copy(phase, i, source, target):
        return pltpu.make_async_remote_copy(
            source.at[chunk(i)], target.at[chunk(i)],
            x_send.at[phase, i], x_recv.at[phase, i],
            device_id=(seg, relay), device_id_type=MESH,
        )

    def env_copy(k):
        return pltpu.make_async_remote_copy(
            built.at[k], env.at[k], env_send.at[k], env_recv.at[k],
            device_id=(nxt, sec), device_id_type=MESH,
        )

    def sum_copies(phase, buffer):
        return [
            pltpu.make_async_remote_copy(
                buffer.at[sec], buffer.at[sec],
                sum_send.at[phase, d], sum_recv.at[phase, d],
                device_id=peers[d], device_id_type=MESH,
            )
            for d in range(secs - 1)
        ]

    def share(phase, buffer, values):
        buffer[sec] = pack(values)
        for copy in sum_copies(phase, buffer):
            copy.start()

    def collect(phase, buffer):
        for copy in sum_copies(phase, buffer):
            copy.wait()

    def entry(buffer, s, k):
        return buffer[s, pl.ds(k, 1), pl.ds(0, 1)]

    def summed(buffer, k):
        value = entry(buffer, 0, k)
        for s in range(1, secs):
            value = value + entry(buffer, s, k)
        return value

    live_rows, live_cols = table_ref[0, 0], table_ref[0, 1]

    def mask(first, count):
        i = lax.broadcasted_iota(jnp.int32, (count, width), 0) + first
        j = lax.broadcasted_iota(jnp.int32, (count, width), 1)
        return (i < live_rows) & (j < live_cols)

    zero = jnp.zeros((1, 1), jnp.float32)

    def begin(i, norm):
        piece = jnp.where(mask(i * rows, rows), psi_ref[chunk(i)].astype(jnp.float32), 0.0)
        start[chunk(i)] = piece.astype(jnp.bfloat16)
        z_copy(0, i, start, start_z).start()
        return norm + total(piece * piece)

    norm = lax.fori_loop(0, CHUNKS, begin, zero)
    share(0, sums1, [norm])

    site_t[...] = site_ref[...].T

    def build(k, _):
        def left(b, _):
            block = pl.ds(pl.multiple_of(b * half, half), half)
            part[block] = dot(terms_ref[k, block], site_ref[...]).astype(jnp.bfloat16)
            return 0

        lax.fori_loop(0, 2, left, 0)

        def right(b, _):
            block = pl.ds(pl.multiple_of(b * half, half), half)
            built[k, block] = dot(site_t[block], part[...]).astype(jnp.bfloat16)
            return 0

        lax.fori_loop(0, 2, right, 0)
        env_copy(k).start()
        return 0

    lax.fori_loop(0, 3, build, 0)

    collect(0, sums1)
    scale = 1.0 / jnp.sqrt(summed(sums1, 0) + eps)
    has_env = jnp.where(seg > 0, 1.0, 0.0).astype(jnp.float32)
    has_x = jnp.where((sec > 0) & (sec < secs - 1), 1.0, 0.0).astype(jnp.float32)

    def scaled(i, source, target):
        piece = (source[chunk(i)].astype(jnp.float32) * scale).astype(jnp.bfloat16)
        target[chunk(i)] = piece
        return piece

    def own(i, _):
        scaled(i, start, vec)
        return 0

    lax.fori_loop(0, CHUNKS, own, 0)

    right_z, right_x = right_ref.at[1 - parity], right_ref.at[parity]
    env_z, env_x = env.at[2 - parity], env.at[1 + parity]

    def relay_z(phase, i, source, target_z, target_x):
        z_copy(phase, i, source, target_z).wait_recv()
        x_copy(phase, i, target_z, target_x).start()

    def first_z(i):
        low_z[chunk(i)] = dot(scaled(i, start_z, vec_z), right_z[...]).astype(jnp.bfloat16)

    def first_x(i):
        x_copy(0, i, start_z, start_x).wait_recv()
        low_x[chunk(i)] = (dot(scaled(i, start_x, vec_x), right_x[...]) * has_x).astype(jnp.bfloat16)

    relay_z(0, 0, start, start_z, start_x)
    first_z(0)

    def arrive(i, _):
        relay_z(0, i, start, start_z, start_x)
        first_z(i)
        first_x(i - 1)
        return 0

    lax.fori_loop(1, CHUNKS, arrive, 0)
    first_x(CHUNKS - 1)
    for k in range(3):
        env_copy(k).wait_recv()

    def apply(b, sums):
        block = pl.ds(pl.multiple_of(b * half, half), half)
        value = dot(env[0, block], vec[...])
        value += dot(env_z[block], low_z[...])
        value += dot(env_x[block], low_x[...])
        value = jnp.where(mask(b * half, half), value * has_env, 0.0)
        image[block] = value
        mine = vec[block].astype(jnp.float32)
        return sums[0] + total(mine * value), sums[1] + total(mine * mine)

    along, size = lax.fori_loop(0, 2, apply, (zero, zero))
    ratio = jnp.where(size > 0.0, along / jnp.where(size > 0.0, size, 1.0), 0.0)

    def reduce(i, sums):
        mine = vec[chunk(i)].astype(jnp.float32)
        piece = image[chunk(i)] - ratio * mine
        image[chunk(i)] = piece
        resid[chunk(i)] = piece.astype(jnp.bfloat16)
        z_copy(1, i, resid, resid_z).start()
        return sums[0] + total(piece * piece), sums[1] + total(mine * piece)

    rho, cross = lax.fori_loop(0, CHUNKS, reduce, (zero, zero))
    share(1, sums2, [along, size, rho, cross, ratio])
    collect(1, sums2)
    alpha = summed(sums2, 0)
    beta_sq = zero
    for s in range(secs):
        delta = entry(sums2, s, 4) - alpha
        beta_sq = beta_sq + entry(sums2, s, 2) + 2.0 * delta * entry(sums2, s, 3)
        beta_sq = beta_sq + delta * delta * entry(sums2, s, 1)
    beta = jnp.sqrt(jnp.maximum(beta_sq, 0.0) + eps)
    inverse = 1.0 / beta
    shift_own = ratio - alpha
    shift_z = entry(sums2, partner, 4) - alpha
    shift_x = entry(sums2, origin, 4) - alpha

    def second(i, sums):
        mine = vec[chunk(i)].astype(jnp.float32)
        piece = ((image[chunk(i)] + shift_own * mine) * inverse).astype(jnp.bfloat16)
        start[chunk(i)] = piece
        wide = piece.astype(jnp.float32)
        return sums[0] + total(mine * wide), sums[1] + total(wide * wide)

    for i in range(CHUNKS):
        z_copy(0, i, start, start_z).wait_send()
    overlap, size2 = lax.fori_loop(0, CHUNKS, second, (zero, zero))

    def adjoint(b, gamma):
        block = pl.ds(pl.multiple_of(b * half, half), half)
        adj_z[block] = dot_t(env_z[:, block], start[...])
        adj_x[block] = dot_t(env_x[:, block], start[...])
        return gamma + total(start[block].astype(jnp.float32) * dot(env[0, block], start[...]))

    gamma = zero
    for b in range(2):
        gamma = adjoint(b, gamma)

    def second_term(i, source, base, shift, matrix, adj):
        piece = source[chunk(i)].astype(jnp.float32) + shift * base[chunk(i)].astype(jnp.float32)
        piece = (piece * inverse).astype(jnp.bfloat16)
        low = dot(piece, matrix[...]).astype(jnp.bfloat16).astype(jnp.float32)
        return total(low * adj[chunk(i)])

    def second_z(i):
        return second_term(i, resid_z, vec_z, shift_z, right_z, adj_z)

    def second_x(i):
        x_copy(1, i, resid_z, resid_x).wait_recv()
        return second_term(i, resid_x, vec_x, shift_x, right_x, adj_x) * has_x

    relay_z(1, 0, resid, resid_z, resid_x)
    gamma = gamma + second_z(0)

    def arrive2(i, gamma):
        relay_z(1, i, resid, resid_z, resid_x)
        return gamma + second_z(i) + second_x(i - 1)

    gamma = lax.fori_loop(1, CHUNKS, arrive2, gamma)
    gamma = (gamma + second_x(CHUNKS - 1)) * has_env

    share(2, sums3, [gamma, size, overlap, size2])
    collect(2, sums3)
    gamma = summed(sums3, 0)
    lowest = 0.5 * (alpha + gamma) - jnp.sqrt(0.25 * (alpha - gamma) ** 2 + beta**2)
    first = gamma - lowest
    united_sq = (
        first * first * summed(sums3, 1)
        - 2.0 * first * beta * summed(sums3, 2)
        + beta * beta * summed(sums3, 3)
    )
    factor = math.sqrt(secs * width * width) / jnp.sqrt(jnp.maximum(united_sq, 0.0) + eps)

    def finish(i, _):
        united = first * vec[chunk(i)].astype(jnp.float32) - beta * start[chunk(i)].astype(jnp.float32)
        ground_ref[chunk(i)] = (united * factor).astype(jnp.bfloat16)
        return 0

    lax.fori_loop(0, CHUNKS, finish, 0)

    for i in range(CHUNKS):
        x_copy(0, i, start_z, start_x).wait_send()
        x_copy(1, i, resid_z, resid_x).wait_send()
        z_copy(1, i, resid, resid_z).wait_send()
    for k in range(3):
        env_copy(k).wait_send()


def lanczos(table, psi, site, terms, right, secs):
    width = psi.shape[0]
    square = (width, width)
    bf = functools.partial(pltpu.VMEM, dtype=jnp.bfloat16)
    blocks = lambda *lead: pltpu.VMEM((*lead, *square), jnp.bfloat16)
    wide = pltpu.VMEM(square, jnp.float32)
    sums = pltpu.VMEM((secs, 8, 128), jnp.float32)
    dma = pltpu.SemaphoreType.DMA
    vmem = pl.BlockSpec(memory_space=pltpu.VMEM)
    return pl.pallas_call(
        lanczos_kernel,
        out_shape=jax.ShapeDtypeStruct(square, jnp.bfloat16),
        in_specs=[pl.BlockSpec(memory_space=pltpu.SMEM)] + [vmem] * 4,
        out_specs=vmem,
        scratch_shapes=[
            blocks(), blocks(), blocks(), blocks(), blocks(), blocks(3), blocks(3),
            blocks(), blocks(), blocks(), blocks(), blocks(), wide,
            blocks(), blocks(), blocks(), wide, wide,
            sums, sums, sums,
            dma((2, CHUNKS)), dma((2, CHUNKS)), dma((2, CHUNKS)), dma((2, CHUNKS)),
            dma((3,)), dma((3,)), dma((3, secs)), dma((3, secs)),
        ],
        compiler_params=pltpu.CompilerParams(
            collective_id=1, has_side_effects=True, vmem_limit_bytes=40 * 2**20
        ),
        cost_estimate=pl.CostEstimate(flops=16 * 2 * width**3, bytes_accessed=8 * width**2, transcendentals=0),
    )(table, psi, site, terms, right)


def product(left, right):
    return jnp.dot(left, right, preferred_element_type=jnp.float32)


def per_device(psi_start, left_site, left_terms, right_terms, start_cols, sector_table):
    cols = start_cols[0]
    table = sector_table[0]
    width = psi_start.shape[-1]
    kept_cols = cols.shape[1]
    keep = (jnp.arange(kept_cols, dtype=jnp.int32) < table[2]).astype(jnp.float32)
    ground = lanczos(
        sector_table, psi_start[0, 0], left_site[0, 0], left_terms[0, 0], right_terms[0, 0],
        lax.axis_size("sec"),
    )
    ranged = (product(ground, cols) * keep[None, :]).astype(jnp.bfloat16)
    rangef = ranged.astype(jnp.float32)
    gram = product(ranged.T, ranged) + jnp.eye(kept_cols, dtype=jnp.float32) * (1.0 - keep)[None, :]
    factors = jnp.linalg.cholesky(gram)
    solved = jax.scipy.linalg.solve_triangular(factors, rangef.T, lower=True)
    basis = solved.T.astype(jnp.bfloat16)
    coeff = product(basis.T, ground).astype(jnp.bfloat16)
    kept = product(basis, coeff).astype(jnp.bfloat16)
    dens = (product(kept, kept.T) / width).astype(jnp.bfloat16)
    segs = lax.axis_size("seg")
    back = lax.ppermute(dens, "seg", [(i + 1, i) for i in range(segs - 1)])
    return (kept[None, None], back[None, None])


def solution(mesh):
    placed = (
        P("seg", "sec", None, None),
        P("seg", "sec", None, None),
        P("seg", "sec", None, None, None),
        P("seg", "sec", None, None, None),
        P("sec", None, None),
        P("sec", None),
    )
    return jax.shard_map(
        per_device,
        mesh=mesh,
        in_specs=placed,
        out_specs=(P("seg", "sec", None, None), P("seg", "sec", None, None)),
        check_vma=False,
    )
```

time: 510 us -> 250 us (0.49)
  the two profiles are of different devices: /device:TPU:1 before, /device:TPU:24 now
where the time goes in v1:
time: 250 us; the launch traced here: 249 us
  Pallas kernels  140 us (56%)
  other arithmetic  55.3 us (22%)
  starting transfers between devices  30 us (12%)
  local copies, waits for them, and re-layouts  11.6 us (5%)
  waiting for transfers between devices  6.68 us (3%)
  matrix products  3.38 us (1%)
    pallas_call x1, Pallas kernels, lanczos(): pl.pallas_call(lanczos_kernel, out_shape=jax.ShapeDtypeStruct(square, jnp...  140 us
    another operation x6, other arithmetic, per_device(): factors = jnp.linalg.cholesky(gram)  34 us
    ppermute x1, starting transfers between devices, per_device(): back = lax.ppermute(dens, 'seg', [(i + 1, i) for i in range(segs - 1)])  30 us
    another operation x3, other arithmetic, per_device(): solved = jax.scipy.linalg.solve_triangular(factors, rangef.T, lower=True)  19.9 us
    ppermute x1, waiting for transfers between devices, per_device(): back = lax.ppermute(dens, 'seg', [(i + 1, i) for i in range(segs - 1)])  6.68 us
    unnamed x15, local copies, waits for them, and re-layouts  6.17 us
  transfers between devices with their start and end apart: 1, of which 1 were waited for; matrix products, arithmetic and copies ran while one was open for 0% of the time, Pallas kernels for 0%

profile of v1, /device:TPU:24, one launch (start us, length us, event | category | flops | bytes accessed | tf_op | source)
XLA Modules:
  0.0 249.1 jit_solution(10354801851678016541)
XLA Ops:
  0.6 1.3 slice.52
  1.9 0.6 compare_convert_fusion
  2.6 0.7 broadcast_subtract_fusion
  3.3 1.4 copy-done.1
  4.7 1.2 copy-done.2
  5.9 1.0 copy-done.3
  6.9 1.0 copy-done.4
  8.0 0.7 copy-done.5
  8.6 140.1 %shard_map.77 = bf16[512,512]{1,0:T(8,128)(2,1)S(1)} custom-call(s32[1,3]{1,0:T(1,128)S(1)} %copy-done.5, bf16[512,512]{1,0:T(8,128)(2,1)S(1)} %bitcast.54, bf16[512,512]{1,0:T(8,128)(2,1)S(1)} %bitcast.55, bf16[3,512,512]{2,1,0:T(8,128)(2,1)S(1)} %bitcast.52, bf16[2,512,512]{2,1,0:T(8,128)(2,1)S(1)} %bitcast.53), custom_call_target="tpu_custom_call" | custom-call | flops 4294967296 | bytes 2097152 | tf_op jit(solution)/shard_map/pallas_call | solution.py:313
  149.6 11.7 %cholesky.49 = f32[128,128]{1,0:T(8,128)S(1)} custom-call(f32[128,128]{1,0:T(8,128)S(1)} %cholesky.115), custom_call_target="Cholesky" | custom-call | tf_op jit(solution)/shard_map/jit(cholesky)/cholesky | solution.py:350
  161.3 9.8 %custom-call.15 = f32[1,128,128]{1,2,0:T(8,128)S(1)} custom-call(f32[1,128,128]{2,1,0:T(8,128)S(1)} %get-tuple-element.23), custom_call_target="InvertDiagBlocksLowerTriangular" | custom-call | tf_op jit(solution)/shard_map/jit(cholesky)/cholesky | solution.py:350
  171.6 11.7 %cholesky.103 = f32[128,128]{1,0:T(8,128)S(1)} custom-call(f32[128,128]{1,0:T(8,128)S(1)} %convolution_subtract_fusion.1), custom_call_target="Cholesky" | custom-call | tf_op jit(solution)/shard_map/jit(cholesky)/cholesky | solution.py:350
  183.4 0.7 compare_reduce_fusion
  185.4 3.9 %while.1 = (s32[]{:T(128)}, f32[256,256]{1,0:T(8,128)S(1)}, s32[2,2]{1,0:T(2,128)S(1)}, f32[2,128,128]{2,1,0:T(8,128)S(1)}, s32[]{:T(128)}) while((s32[]{:T(128)}, f32[256,256]{1,0:T(8,128)S(1)}, s32[2,2]{1,0:T(2,128)S(1)}, f32[2,128,128]{2,1,0:T(8,128)S(1)}, s32[]{:T(128)}) %tuple.28), condition=%wide.while_cond, body=%wide.while_body.sunk | while | flops 2 | bytes 131181 | solution.py:351
  185.4 0.6 fusion.33
  186.0 1.3 bitcast_dynamic-update-slice_fusion.2
  187.4 0.6 fusion.33
  188.0 1.3 bitcast_dynamic-update-slice_fusion.2
  189.3 19.9 %custom-call.16 = f32[2,128,128]{1,2,0:T(8,128)S(1)} custom-call(f32[2,128,128]{2,1,0:T(8,128)S(1)} %get-tuple-element.9), custom_call_target="InvertDiagBlocksLowerTriangular" | custom-call | tf_op jit(solution)/shard_map/jit(_solve_triangular)/triangular_solve | solution.py:351
  209.6 0.6 convolution_subtract_fusion
  210.6 0.6 convolution_convert_fusion
  211.6 30.0 %collective-permute-start = (bf16[512,512]{1,0:T(8,128)(2,1)S(1)}, bf16[512,512]{1,0:T(8,128)(2,1)S(1)}, u32[]{:S(2)}, u32[]{:S(2)}) collective-permute-start(bf16[512,512]{1,0:T(8,128)(2,1)S(1)} %fusion), channel_id=1, source_target_pairs={{8,0},{16,8},{24,16},{32,24},{40,32},{48,40},{56,48},{64,56},{72,6... | collective-permute-start | bytes 1572872 | tf_op jit(solution)/shard_map/ppermute | solution.py:357
  241.6 6.7 %collective-permute-done = bf16[512,512]{1,0:T(8,128)(2,1)S(1)} collective-permute-done((bf16[512,512]{1,0:T(8,128)(2,1)S(1)}, bf16[512,512]{1,0:T(8,128)(2,1)S(1)}, u32[]{:S(2)}, u32[]{:S(2)}) %collective-permute-start) | collective-permute-done | bytes 524320 | tf_op jit(solution)/shard_map/ppermute | solution.py:357
  248.3 0.8 copy.21
  (28 shorter events, 2.7 us)
Async XLA Ops:
  0.6 148.1 %copy-start = (bf16[1,512,256]{2,1,0:T(8,128)(2,1)S(1)}, bf16[1,512,256]{2,1,0:T(8,128)(2,1)}, u32[]{:S(2)}) copy-start(bf16[1,512,256]{2,1,0:T(8,128)(2,1)} %param.10) | copy-start | bytes 786436
  3.3 1.4 copy-start.1
  4.7 1.2 copy-start.2
  5.9 1.0 copy-start.3
  6.9 1.0 copy-start.4
  8.0 0.7 copy-start.5
  211.2 37.9 %copy-start.6 = (bf16[512,512]{1,0:T(8,128)(2,1)}, bf16[512,512]{1,0:T(8,128)(2,1)S(1)}, u32[]{:S(2)}) copy-start(bf16[512,512]{1,0:T(8,128)(2,1)S(1)} %convolution_convert_fusion) | copy-start | bytes 1572868
  211.6 36.7 %collective-permute-start = (bf16[512,512]{1,0:T(8,128)(2,1)S(1)}, bf16[512,512]{1,0:T(8,128)(2,1)S(1)}, u32[]{:S(2)}, u32[]{:S(2)}) collective-permute-start(bf16[512,512]{1,0:T(8,128)(2,1)S(1)} %fusion), channel_id=1, source_target_pairs={{8,0},{16,8},{24,16},{32,24},{40,32},{48,40},{56,48},{64,56},{72,6... | collective-permute-start | bytes 1572872 | tf_op jit(solution)/shard_map/ppermute | solution.py:357

commit v2 on v1

--- a/solution.py
+++ b/solution.py
@@ -330,29 +330,129 @@
     )(table, psi, site, terms, right)
 
 
-def product(left, right):
-    return jnp.dot(left, right, preferred_element_type=jnp.float32)
+def fdot(left, right):
+    return jnp.dot(left, right, precision=lax.Precision.HIGHEST, preferred_element_type=jnp.float32)
+
+
+def spread_lane(tile, lane):
+    return jnp.broadcast_to(tile[:, lane : lane + 1], tile.shape)
+
+
+def spread_row(tile, row):
+    return jnp.broadcast_to(tile[row : row + 1, :], tile.shape)
+
+
+def invert_factor(block, panel):
+    size = block.shape[0]
+    count = size // 8
+    tiles = [block[8 * t : 8 * t + 8] for t in range(count)]
+    lane = lax.broadcasted_iota(jnp.int32, (8, size), 1)
+    sub = lax.broadcasted_iota(jnp.int32, (8, size), 0)
+    scales = [None] * count
+    for j in range(0, size, panel):
+        top, base = j // 8, j % 8
+        cols = [
+            {t: spread_lane(tiles[t], j + c) for t in range(top, count)} for c in range(panel)
+        ]
+        inside = (lane >= j) & (lane < j + panel)
+        for t in range(top, count):
+            tiles[t] = jnp.where(inside, jnp.where((lane - j == sub + 8 * t - j) , 1.0, 0.0) if t == top else 0.0, tiles[t])
+        for c in range(panel):
+            row = base + c
+            pivot = spread_row(cols[c][top], row)
+            inverse = 1.0 / pivot
+            scale = lax.rsqrt(pivot)
+            scales[top] = scale if scales[top] is None else jnp.where(sub >= row, scale, scales[top])
+            below = sub > row
+            factor = {}
+            for t in range(top, count):
+                f = cols[c][t] * inverse
+                factor[t] = jnp.where(below, f, 0.0) if t == top else f
+            for d in range(c + 1, panel):
+                head = spread_row(cols[d][top], row)
+                for t in range(top, count):
+                    cols[d][t] = cols[d][t] - factor[t] * head
+            line = spread_row(tiles[top], row)
+            for t in range(top, count):
+                tiles[t] = tiles[t] - factor[t] * line
+    out = [tiles[t] * scales[t] for t in range(count)]
+    full = jnp.concatenate(out, axis=0)
+    r = lax.broadcasted_iota(jnp.int32, (size, size), 0)
+    q = lax.broadcasted_iota(jnp.int32, (size, size), 1)
+    return jnp.where(r >= q, full, 0.0)
+
+
+def split_dot(left, right):
+    result = None
+    rest = left
+    for _ in range(3):
+        part = rest.astype(jnp.bfloat16)
+        rest = rest - part.astype(jnp.float32)
+        term = dot(part, right)
+        result = term if result is None else result + term
+    return result
+
+
+def truncate_kernel(table_ref, ground_ref, cols_ref, kept_ref, dens_ref, basis, basis_t, range_t, gram, inv):
+    width, rank = cols_ref.shape
+    half = rank // 2
+    lane = lax.broadcasted_iota(jnp.int32, (1, rank), 1)
+    keep = jnp.where(lane < table_ref[0, 2], 1.0, 0.0)
+    for b in range(2):
+        block = pl.ds(b * 256, 256)
+        rng = (dot(ground_ref[block], cols_ref[...]) * keep).astype(jnp.bfloat16)
+        basis[block] = rng
+        range_t[:, block] = rng.T
+    row = lax.broadcasted_iota(jnp.int32, (rank, rank), 0)
+    col = lax.broadcasted_iota(jnp.int32, (rank, rank), 1)
+    gram[...] = dot(range_t[...], basis[...]) + jnp.where((row == col) & (col >= table_ref[0, 2]), 1.0, 0.0)
+    first = invert_factor(gram[:half, :half], 8)
+    upper = fdot(first, gram[:half, half:])
+    upper_t = upper.T
+    second = invert_factor(gram[half:, half:] - fdot(upper_t, upper), 8)
+    inv[:half, :half] = first
+    inv[:half, half:] = jnp.zeros((half, half), jnp.float32)
+    inv[half:, :half] = -fdot(second, fdot(upper_t, first))
+    inv[half:, half:] = second
+    basis_t[...] = split_dot(inv[...], range_t[...]).astype(jnp.bfloat16)
+    basis[...] = basis_t[...].T
+    coeff = dot(basis_t[...], ground_ref[...]).astype(jnp.bfloat16)
+    for b in range(2):
+        block = pl.ds(b * 256, 256)
+        kept_ref[block] = dot(basis[block], coeff).astype(jnp.bfloat16)
+    kept_t = kept_ref[...].T
+    for b in range(2):
+        block = pl.ds(b * 256, 256)
+        dens_ref[block] = (dot(kept_ref[block], kept_t) * (1.0 / width)).astype(jnp.bfloat16)
+
+
+def truncate(table, ground, cols):
+    width, rank = cols.shape
+    square = jax.ShapeDtypeStruct((width, width), jnp.bfloat16)
+    vmem = pl.BlockSpec(memory_space=pltpu.VMEM)
+    return pl.pallas_call(
+        truncate_kernel,
+        out_shape=(square, square),
+        in_specs=[pl.BlockSpec(memory_space=pltpu.SMEM), vmem, vmem],
+        out_specs=(vmem, vmem),
+        scratch_shapes=[
+            pltpu.VMEM((width, rank), jnp.bfloat16),
+            pltpu.VMEM((rank, width), jnp.bfloat16),
+            pltpu.VMEM((rank, width), jnp.bfloat16),
+            pltpu.VMEM((rank, rank), jnp.float32),
+            pltpu.VMEM((rank, rank), jnp.float32),
+        ],
+        compiler_params=pltpu.CompilerParams(vmem_limit_bytes=24 * 2**20),
+        cost_estimate=pl.CostEstimate(flops=2 * width**3 * 3, bytes_accessed=3 * width**2, transcendentals=0),
+    )(table, ground, cols)
 
 
 def per_device(psi_start, left_site, left_terms, right_terms, start_cols, sector_table):
-    cols = start_cols[0]
-    table = sector_table[0]
-    width = psi_start.shape[-1]
-    kept_cols = cols.shape[1]
-    keep = (jnp.arange(kept_cols, dtype=jnp.int32) < table[2]).astype(jnp.float32)
     ground = lanczos(
         sector_table, psi_start[0, 0], left_site[0, 0], left_terms[0, 0], right_terms[0, 0],
         lax.axis_size("sec"),
     )
-    ranged = (product(ground, cols) * keep[None, :]).astype(jnp.bfloat16)
-    rangef = ranged.astype(jnp.float32)
-    gram = product(ranged.T, ranged) + jnp.eye(kept_cols, dtype=jnp.float32) * (1.0 - keep)[None, :]
-    factors = jnp.linalg.cholesky(gram)
-    solved = jax.scipy.linalg.solve_triangular(factors, rangef.T, lower=True)
-    basis = solved.T.astype(jnp.bfloat16)
-    coeff = product(basis.T, ground).astype(jnp.bfloat16)
-    kept = product(basis, coeff).astype(jnp.bfloat16)
-    dens = (product(kept, kept.T) / width).astype(jnp.bfloat16)
+    kept, dens = truncate(sector_table, ground, start_cols[0])
     segs = lax.axis_size("seg")
     back = lax.ppermute(dens, "seg", [(i + 1, i) for i in range(segs - 1)])
     return (kept[None, None], back[None, None])

time: 250 us -> 195 us (0.78)
  other arithmetic: 55.3 us -> 0 us
  Pallas kernels: 140 us -> 152 us
  local copies, waits for them, and re-layouts: 11.6 us -> 6.16 us
  matrix products: 3.38 us -> 0 us
    another operation x9 -> x0, other arithmetic: 53.9 us -> none  [the longest x6 34 us: per_device(): factors = jnp.linalg.cholesky(gram)]
    pallas_call x0 -> x1, Pallas kernels: none -> 11.7 us  [truncate(): pl.pallas_call(truncate_kernel, out_shape=(square, square), in_specs=[pl....]
    another operation x9 -> x0, local copies, waits for them, and re-layouts: 3.97 us -> none
    unnamed x15 -> x13, local copies, waits for them, and re-layouts: 6.17 us -> 6.16 us
where the time goes in v2:
time: 195 us
  Pallas kernels  152 us (78%)
  starting transfers between devices  29.8 us (15%)
  waiting for transfers between devices  6.68 us (3%)
  local copies, waits for them, and re-layouts  6.16 us (3%)
    pallas_call x1, Pallas kernels, lanczos(): pl.pallas_call(lanczos_kernel, out_shape=jax.ShapeDtypeStruct(square, jnp...  140 us
    ppermute x1, starting transfers between devices, per_device(): back = lax.ppermute(dens, 'seg', [(i + 1, i) for i in range(segs - 1)])  29.8 us
    pallas_call x1, Pallas kernels, truncate(): pl.pallas_call(truncate_kernel, out_shape=(square, square), in_specs=[pl....  11.7 us
    ppermute x1, waiting for transfers between devices, per_device(): back = lax.ppermute(dens, 'seg', [(i + 1, i) for i in range(segs - 1)])  6.68 us
    unnamed x13, local copies, waits for them, and re-layouts  6.16 us
  transfers between devices with their start and end apart: 1, of which 1 were waited for; matrix products, arithmetic and copies ran while one was open for 0% of the time, Pallas kernels for 0%

profile of v2, /device:TPU:24, one launch (start us, length us, event | category | flops | bytes accessed | tf_op | source)
XLA Modules:
  0.0 195.2 jit_solution(5629183847769116530)
XLA Ops:
  0.6 0.0 copy-start
  0.6 1.4 copy-done
  2.0 0.0 copy-start.1
  2.0 1.2 copy-done.1
  3.3 0.0 copy-start.2
  3.3 1.0 copy-done.2
  4.3 0.0 copy-start.3
  4.3 1.0 copy-done.3
  5.3 0.0 copy-start.5
  5.4 0.7 copy-done.5
  6.0 0.0 copy-start.4
  6.0 140.1 %shard_map.77.ground_ref = bf16[512,512]{1,0:T(8,128)(2,1)S(1)} custom-call(s32[1,3]{1,0:T(1,128)S(1)} %copy-done.5, bf16[512,512]{1,0:T(8,128)(2,1)S(1)} %bitcast.9, bf16[512,512]{1,0:T(8,128)(2,1)S(1)} %bitcast.10, bf16[3,512,512]{2,1,0:T(8,128)(2,1)S(1)} %bitcast.7, bf16[2,512,512]{2,1,0:T(8,128)(2,1)S(1)} %bitcast.8), custom_call_target="tpu_custom_call" | custom-call | flops 4294967296 | bytes 2097152 | tf_op jit(solution)/shard_map/pallas_call | solution.py:313
  146.1 0.0 copy-done.4
  146.2 11.7 %shard_map.78 = (bf16[512,512]{1,0:T(8,128)(2,1)}, bf16[512,512]{1,0:T(8,128)(2,1)S(1)}) custom-call(s32[1,3]{1,0:T(1,128)S(1)} %copy-done.5, bf16[512,512]{1,0:T(8,128)(2,1)S(1)} %shard_map.77.ground_ref, bf16[512,256]{1,0:T(8,128)(2,1)S(1)} %bitcast.11), custom_call_target="tpu_custom_call" | custom-call | flops 805306368 | bytes 786432 | tf_op jit(solution)/shard_map/pallas_call | solution.py:433
  157.9 29.8 %collective-permute-start = (bf16[512,512]{1,0:T(8,128)(2,1)S(1)}, bf16[512,512]{1,0:T(8,128)(2,1)S(1)}, u32[]{:S(2)}, u32[]{:S(2)}) collective-permute-start(bf16[512,512]{1,0:T(8,128)(2,1)S(1)} %get-tuple-element.5), channel_id=1, source_target_pairs={{8,0},{16,8},{24,16},{32,24},{40,32},{48,40},{56,48},{64,56},{72,6... | collective-permute-start | bytes 1572872 | tf_op jit(solution)/shard_map/ppermute | solution.py:457
  187.7 6.7 %collective-permute-done = bf16[512,512]{1,0:T(8,128)(2,1)S(1)} collective-permute-done((bf16[512,512]{1,0:T(8,128)(2,1)S(1)}, bf16[512,512]{1,0:T(8,128)(2,1)S(1)}, u32[]{:S(2)}, u32[]{:S(2)}) %collective-permute-start) | collective-permute-done | bytes 524320 | tf_op jit(solution)/shard_map/ppermute | solution.py:457
  194.4 0.8 copy.9
Async XLA Ops:
  0.6 1.4 copy-start
  2.0 1.2 copy-start.1
  3.3 1.0 copy-start.2
  4.3 1.0 copy-start.3
  5.3 0.7 copy-start.5
  6.0 140.1 %copy-start.4 = (bf16[1,512,256]{2,1,0:T(8,128)(2,1)S(1)}, bf16[1,512,256]{2,1,0:T(8,128)(2,1)}, u32[]{:S(2)}) copy-start(bf16[1,512,256]{2,1,0:T(8,128)(2,1)} %param.10) | copy-start | bytes 786436
  157.9 36.5 %collective-permute-start = (bf16[512,512]{1,0:T(8,128)(2,1)S(1)}, bf16[512,512]{1,0:T(8,128)(2,1)S(1)}, u32[]{:S(2)}, u32[]{:S(2)}) collective-permute-start(bf16[512,512]{1,0:T(8,128)(2,1)S(1)} %get-tuple-element.5), channel_id=1, source_target_pairs={{8,0},{16,8},{24,16},{32,24},{40,32},{48,40},{56,48},{64,56},{72,6... | collective-permute-start | bytes 1572872 | tf_op jit(solution)/shard_map/ppermute | solution.py:457

commit v3 on v2

v3 whole, which is shorter than its diff:
```python
import math

import jax
import jax.numpy as jnp
from jax import lax
from jax.experimental import pallas as pl
from jax.experimental.pallas import tpu as pltpu
from jax.sharding import PartitionSpec as P

eps = 1e-06
MESH = pl.DeviceIdType.MESH
CHUNKS = 8
ENV_AT = 4
AHEAD = 1


def dot(left, right):
    return jnp.dot(left, right, preferred_element_type=jnp.float32)


def dot_left_t(left, right):
    return lax.dot_general(
        left, right, (((0,), (0,)), ((), ())), preferred_element_type=jnp.float32
    )


def dot_right_t(left, right):
    return lax.dot_general(
        left, right, (((1,), (1,)), ((), ())), preferred_element_type=jnp.float32
    )


def total(block):
    return jnp.sum(jnp.sum(block, axis=0, keepdims=True), axis=1, keepdims=True)


def pack(values):
    lane = lax.broadcasted_iota(jnp.int32, (1, 128), 1)
    row = jnp.zeros((1, 128), jnp.float32)
    for k, value in enumerate(values):
        row = jnp.where(lane == k, value, row)
    return row


def lanczos_kernel(
    table_ref, psi_hbm, site_hbm, terms_hbm, right_hbm, ground_ref,
    psi, site, terms, right,
    start, start_z, start_x, site_t, part, built, env, vec, vec_z,
    low_z, low_x, image, resid, resid_z, ritz, adj, pull, pull_out, pull_in,
    sums1, sums2, sums3,
    load, z_send, z_recv, x_send, x_recv, env_send, env_recv, pull_send, pull_recv, sum_send, sum_recv,
):
    seg, sec = lax.axis_index("seg"), lax.axis_index("sec")
    segs, secs = lax.axis_size("seg"), lax.axis_size("sec")
    width = psi.shape[0]
    rows = width // CHUNKS
    half = width // 2
    parity = lax.rem(sec, 2)
    partner = sec + 1 - 2 * parity
    relay = lax.rem(sec + 2 - 4 * parity + secs, secs)
    source = lax.rem(sec - 2 + 4 * parity + secs, secs)
    nxt, prv = lax.rem(seg + 1, segs), lax.rem(seg + segs - 1, segs)
    peers = [(seg, lax.rem(sec + d, secs)) for d in range(1, secs)]

    barrier = pltpu.get_barrier_semaphore()
    neighbours = peers + [(nxt, sec), (prv, sec)]
    for device in neighbours:
        pl.semaphore_signal(barrier, inc=1, device_id=device, device_id_type=MESH)

    loads = [
        pltpu.make_async_copy(psi_hbm, psi, load.at[0]),
        pltpu.make_async_copy(site_hbm, site, load.at[1]),
        pltpu.make_async_copy(terms_hbm, terms, load.at[2]),
        pltpu.make_async_copy(right_hbm, right, load.at[3]),
    ]
    for copy in loads:
        copy.start()

    def chunk(i):
        return pl.ds(pl.multiple_of(i * rows, rows), rows)

    def halves(b):
        return pl.ds(pl.multiple_of(b * half, half), half)

    def z_copy(phase, i, held, target):
        return pltpu.make_async_remote_copy(
            held.at[chunk(i)], target.at[chunk(i)],
            z_send.at[phase, i], z_recv.at[phase, i],
            device_id=(seg, partner), device_id_type=MESH,
        )

    def x_copy(i):
        return pltpu.make_async_remote_copy(
            start_z.at[chunk(i)], start_x.at[chunk(i)],
            x_send.at[i], x_recv.at[i],
            device_id=(seg, relay), device_id_type=MESH,
        )

    def env_copy(i):
        return pltpu.make_async_remote_copy(
            built.at[:, chunk(i)], env.at[:, chunk(i)], env_send.at[i], env_recv.at[i],
            device_id=(nxt, sec), device_id_type=MESH,
        )

    def pull_copy():
        return pltpu.make_async_remote_copy(
            pull_out, pull_in, pull_send.at[0], pull_recv.at[0],
            device_id=(seg, source), device_id_type=MESH,
        )

    def sum_copies(phase, buffer):
        return [
            pltpu.make_async_remote_copy(
                buffer.at[sec], buffer.at[sec],
                sum_send.at[phase, d], sum_recv.at[phase, d],
                device_id=peers[d], device_id_type=MESH,
            )
            for d in range(secs - 1)
        ]

    def share(phase, buffer):
        for copy in sum_copies(phase, buffer):
            copy.start()

    def collect(phase, buffer):
        for copy in sum_copies(phase, buffer):
            copy.wait()

    def summed(buffer):
        return jnp.sum(jnp.sum(buffer[...], axis=0), axis=0, keepdims=True)

    live_rows, live_cols = table_ref[0, 0], table_ref[0, 1]

    def mask(first, count):
        i = lax.broadcasted_iota(jnp.int32, (count, width), 0) + first
        j = lax.broadcasted_iota(jnp.int32, (count, width), 1)
        return (i < live_rows) & (j < live_cols)

    zero = jnp.zeros((1, 1), jnp.float32)
    blank = jnp.zeros((8, 128), jnp.float32)
    sums1[sec] = blank
    sums3[sec] = blank
    loads[0].wait()

    def begin(i, norm):
        piece = jnp.where(mask(i * rows, rows), psi[chunk(i)].astype(jnp.float32), 0.0)
        start[chunk(i)] = piece.astype(jnp.bfloat16)
        return norm + total(piece * piece)

    norm = lax.fori_loop(0, CHUNKS, begin, zero)
    sums1[sec, pl.ds(0, 1)] = pack([norm])

    pl.semaphore_wait(barrier, len(neighbours))

    share(0, sums1)

    def send_start(i, _):
        z_copy(0, i, start, start_z).start()
        return 0

    lax.fori_loop(0, CHUNKS, send_start, 0)

    loads[1].wait()
    site_t[...] = site[...].T
    loads[2].wait()

    def build(k, _):
        def left(b, _):
            part[halves(b)] = dot(terms[k, halves(b)], site[...]).astype(jnp.bfloat16)
            return 0

        lax.fori_loop(0, 2, left, 0)

        def outer(b, _):
            built[k, halves(b)] = dot(site_t[halves(b)], part[...]).astype(jnp.bfloat16)
            return 0

        lax.fori_loop(0, 2, outer, 0)
        return 0

    lax.fori_loop(0, 3, build, 0)

    loads[3].wait()
    collect(0, sums1)
    scale = 1.0 / jnp.sqrt(summed(sums1)[:, 0:1] + eps)
    has_env = jnp.where(seg > 0, 1.0, 0.0).astype(jnp.float32)
    has_x = jnp.where((sec > 0) & (sec < secs - 1), 1.0, 0.0).astype(jnp.float32)

    def scaled(i, held):
        return (held[chunk(i)].astype(jnp.float32) * scale).astype(jnp.bfloat16)

    def own(i, _):
        vec[chunk(i)] = scaled(i, start)
        return 0

    lax.fori_loop(0, CHUNKS, own, 0)

    right_z, right_x = right.at[1 - parity], right.at[parity]
    env_z, env_x = env.at[2 - parity], env.at[1 + parity]

    def first_z(i):
        z_copy(0, i, start, start_z).wait_recv()
        x_copy(i).start()
        piece = scaled(i, start_z)
        vec_z[chunk(i)] = piece
        low_z[chunk(i)] = dot(piece, right_z[...]).astype(jnp.bfloat16)

    def first_x(i):
        x_copy(i).wait_recv()
        low_x[chunk(i)] = (dot(scaled(i, start_x), right_x[...]) * has_x).astype(jnp.bfloat16)

    def arrive(i, _):
        first_z(i)
        first_x(i - 1)
        return 0

    def arrive_send(i, _):
        env_copy(i - ENV_AT).start()
        return arrive(i, 0)

    first_z(0)
    lax.fori_loop(1, ENV_AT, arrive, 0)
    lax.fori_loop(ENV_AT, CHUNKS, arrive_send, 0)

    def send_env(i, _):
        env_copy(i).start()
        return 0

    lax.fori_loop(CHUNKS - ENV_AT, CHUNKS, send_env, 0)
    first_x(CHUNKS - 1)

    def apply(i, _):
        env_copy(i).wait_recv()
        value = dot(env[0, chunk(i)], vec[...])
        value += dot(env_z[chunk(i)], low_z[...])
        value += dot(env_x[chunk(i)], low_x[...])
        value = jnp.where(mask(i * rows, rows), value * has_env, 0.0)
        mine = vec[chunk(i)].astype(jnp.float32)
        along, size = total(mine * value), total(mine * mine)
        ratio = jnp.where(size > 0.0, along / jnp.where(size > 0.0, size, 1.0), 0.0)
        piece = value - ratio * mine
        image[chunk(i)] = piece
        resid[chunk(i)] = piece.astype(jnp.bfloat16)
        sums2[sec, pl.ds(i, 1)] = pack([along, size, total(piece * piece), total(mine * piece), ratio])
        return 0

    def send_resid(i, _):
        z_copy(1, i, resid, resid_z).start()
        return 0

    def apply_send(i, _):
        apply(i, 0)
        return send_resid(i, 0)

    lax.fori_loop(0, AHEAD, apply_send, 0)
    lax.fori_loop(AHEAD, CHUNKS, apply, 0)
    share(1, sums2)
    lax.fori_loop(AHEAD, CHUNKS, send_resid, 0)
    collect(1, sums2)

    totals = summed(sums2)
    alpha, size = totals[:, 0:1], totals[:, 1:2]
    beta_sq = zero
    for s in range(secs):
        tile = sums2[s]
        delta = tile[:, 4:5] - alpha
        beta_sq = beta_sq + total(tile[:, 2:3] + 2.0 * delta * tile[:, 3:4] + delta * delta * tile[:, 1:2])
    beta = jnp.sqrt(jnp.maximum(beta_sq, 0.0) + eps)
    inverse = 1.0 / beta

    def shift(s, i):
        return sums2[s, pl.ds(i, 1)][:, 4:5] - alpha

    def second(i, sums):
        mine = vec[chunk(i)].astype(jnp.float32)
        piece = ((image[chunk(i)] + shift(sec, i) * mine) * inverse).astype(jnp.bfloat16)
        ritz[chunk(i)] = piece
        wide = piece.astype(jnp.float32)
        return sums[0] + total(mine * wide), sums[1] + total(wide * wide)

    overlap, size2 = lax.fori_loop(0, CHUNKS, second, (zero, zero))

    for b in range(2):
        adj[b * half : (b + 1) * half] = dot_left_t(env_x[:, b * half : (b + 1) * half], ritz[...]).astype(jnp.bfloat16)

    def pull_x(b, _):
        pull_out[halves(b)] = (dot_right_t(adj[halves(b)], right_x[...]) * has_x).astype(jnp.bfloat16)
        return 0

    lax.fori_loop(0, 2, pull_x, 0)
    pull_copy().start()
    for b in range(2):
        adj[b * half : (b + 1) * half] = dot_left_t(env_z[:, b * half : (b + 1) * half], ritz[...]).astype(jnp.bfloat16)

    def pull_z(b, gamma):
        pull[halves(b)] = dot_right_t(adj[halves(b)], right_z[...])
        return gamma + total(ritz[halves(b)].astype(jnp.float32) * dot(env[0, halves(b)], ritz[...]))

    gamma = lax.fori_loop(0, 2, pull_z, zero)
    pull_copy().wait_recv()

    def join(i, partial):
        both = pull[chunk(i)] + pull_in[chunk(i)].astype(jnp.float32)
        pull[chunk(i)] = both
        return partial + shift(partner, i) * total(both * vec_z[chunk(i)].astype(jnp.float32))

    cross = lax.fori_loop(0, CHUNKS, join, zero)

    def meet(i, partial):
        z_copy(1, i, resid, resid_z).wait_recv()
        return partial + total(pull[chunk(i)] * resid_z[chunk(i)].astype(jnp.float32))

    cross = lax.fori_loop(0, CHUNKS, meet, cross)
    gamma = (gamma + cross * inverse) * has_env
    sums3[sec, pl.ds(0, 1)] = pack([gamma, overlap, size2])
    share(2, sums3)
    collect(2, sums3)
    totals = summed(sums3)
    gamma = totals[:, 0:1]
    lowest = 0.5 * (alpha + gamma) - jnp.sqrt(0.25 * (alpha - gamma) ** 2 + beta * beta)
    first = gamma - lowest
    united_sq = (
        first * first * size - 2.0 * first * beta * totals[:, 1:2] + beta * beta * totals[:, 2:3]
    )
    factor = math.sqrt(secs * width * width) / jnp.sqrt(jnp.maximum(united_sq, 0.0) + eps)

    def finish(i, _):
        united = first * vec[chunk(i)].astype(jnp.float32) - beta * ritz[chunk(i)].astype(jnp.float32)
        ground_ref[chunk(i)] = (united * factor).astype(jnp.bfloat16)
        return 0

    lax.fori_loop(0, CHUNKS, finish, 0)

    def drain(i, _):
        z_copy(0, i, start, start_z).wait_send()
        z_copy(1, i, resid, resid_z).wait_send()
        x_copy(i).wait_send()
        env_copy(i).wait_send()
        return 0

    lax.fori_loop(0, CHUNKS, drain, 0)
    pull_copy().wait_send()


def lanczos(table, psi, site, terms, right, secs):
    width = psi.shape[0]
    square = (width, width)
    blocks = lambda *lead: pltpu.VMEM((*lead, *square), jnp.bfloat16)
    wide = pltpu.VMEM(square, jnp.float32)
    sums = pltpu.VMEM((secs, 8, 128), jnp.float32)
    dma = pltpu.SemaphoreType.DMA
    return pl.pallas_call(
        lanczos_kernel,
        out_shape=jax.ShapeDtypeStruct(square, jnp.bfloat16),
        in_specs=[pl.BlockSpec(memory_space=pltpu.SMEM)] + [pl.BlockSpec(memory_space=pl.ANY)] * 4,
        out_specs=pl.BlockSpec(memory_space=pltpu.VMEM),
        scratch_shapes=[
            blocks(), blocks(), blocks(3), blocks(2),
            blocks(), blocks(), blocks(), blocks(), blocks(), blocks(3), blocks(3), blocks(), blocks(),
            blocks(), blocks(), wide, blocks(), blocks(), blocks(), blocks(), wide, blocks(), blocks(),
            sums, sums, sums,
            dma((4,)), dma((2, CHUNKS)), dma((2, CHUNKS)), dma((CHUNKS,)), dma((CHUNKS,)),
            dma((CHUNKS,)), dma((CHUNKS,)), dma((1,)), dma((1,)), dma((3, secs)), dma((3, secs)),
        ],
        compiler_params=pltpu.CompilerParams(
            collective_id=1, has_side_effects=True, vmem_limit_bytes=62 * 2**20
        ),
        cost_estimate=pl.CostEstimate(flops=16 * 2 * width**3, bytes_accessed=8 * width**2, transcendentals=0),
    )(table, psi, site, terms, right)


def fdot(left, right):
    return jnp.dot(left, right, precision=lax.Precision.HIGHEST, preferred_element_type=jnp.float32)


def spread_lane(tile, lane):
    return jnp.broadcast_to(tile[:, lane : lane + 1], tile.shape)


def spread_row(tile, row):
    return jnp.broadcast_to(tile[row : row + 1, :], tile.shape)


def invert_factor(block, panel):
    size = block.shape[0]
    count = size // 8
    tiles = [block[8 * t : 8 * t + 8] for t in range(count)]
    lane = lax.broadcasted_iota(jnp.int32, (8, size), 1)
    sub = lax.broadcasted_iota(jnp.int32, (8, size), 0)
    scales = [None] * count
    for j in range(0, size, panel):
        top, base = j // 8, j % 8
        cols = [
            {t: spread_lane(tiles[t], j + c) for t in range(top, count)} for c in range(panel)
        ]
        inside = (lane >= j) & (lane < j + panel)
        for t in range(top, count):
            tiles[t] = jnp.where(inside, jnp.where((lane - j == sub + 8 * t - j) , 1.0, 0.0) if t == top else 0.0, tiles[t])
        for c in range(panel):
            row = base + c
            pivot = spread_row(cols[c][top], row)
            inverse = 1.0 / pivot
            scale = lax.rsqrt(pivot)
            scales[top] = scale if scales[top] is None else jnp.where(sub >= row, scale, scales[top])
            below = sub > row
            factor = {}
            for t in range(top, count):
                f = cols[c][t] * inverse
                factor[t] = jnp.where(below, f, 0.0) if t == top else f
            for d in range(c + 1, panel):
                head = spread_row(cols[d][top], row)
                for t in range(top, count):
                    cols[d][t] = cols[d][t] - factor[t] * head
            line = spread_row(tiles[top], row)
            for t in range(top, count):
                tiles[t] = tiles[t] - factor[t] * line
    out = [tiles[t] * scales[t] for t in range(count)]
    full = jnp.concatenate(out, axis=0)
    r = lax.broadcasted_iota(jnp.int32, (size, size), 0)
    q = lax.broadcasted_iota(jnp.int32, (size, size), 1)
    return jnp.where(r >= q, full, 0.0)


def split_dot(left, right):
    result = None
    rest = left
    for _ in range(3):
        part = rest.astype(jnp.bfloat16)
        rest = rest - part.astype(jnp.float32)
        term = dot(part, right)
        result = term if result is None else result + term
    return result


def truncate_kernel(table_ref, ground_ref, cols_ref, kept_ref, dens_ref, basis, basis_t, range_t, gram, inv):
    width, rank = cols_ref.shape
    half = rank // 2
    lane = lax.broadcasted_iota(jnp.int32, (1, rank), 1)
    keep = jnp.where(lane < table_ref[0, 2], 1.0, 0.0)
    for b in range(2):
        block = pl.ds(b * 256, 256)
        rng = (dot(ground_ref[block], cols_ref[...]) * keep).astype(jnp.bfloat16)
        basis[block] = rng
        range_t[:, block] = rng.T
    row = lax.broadcasted_iota(jnp.int32, (rank, rank), 0)
    col = lax.broadcasted_iota(jnp.int32, (rank, rank), 1)
    gram[...] = dot(range_t[...], basis[...]) + jnp.where((row == col) & (col >= table_ref[0, 2]), 1.0, 0.0)
    first = invert_factor(gram[:half, :half], 8)
    upper = fdot(first, gram[:half, half:])
    upper_t = upper.T
    second = invert_factor(gram[half:, half:] - fdot(upper_t, upper), 8)
    inv[:half, :half] = first
    inv[:half, half:] = jnp.zeros((half, half), jnp.float32)
    inv[half:, :half] = -fdot(second, fdot(upper_t, first))
    inv[half:, half:] = second
    basis_t[...] = split_dot(inv[...], range_t[...]).astype(jnp.bfloat16)
    basis[...] = basis_t[...].T
    coeff = dot(basis_t[...], ground_ref[...]).astype(jnp.bfloat16)
    for b in range(2):
        block = pl.ds(b * 256, 256)
        kept_ref[block] = dot(basis[block], coeff).astype(jnp.bfloat16)
    kept_t = kept_ref[...].T
    for b in range(2):
        block = pl.ds(b * 256, 256)
        dens_ref[block] = (dot(kept_ref[block], kept_t) * (1.0 / width)).astype(jnp.bfloat16)


def truncate(table, ground, cols):
    width, rank = cols.shape
    square = jax.ShapeDtypeStruct((width, width), jnp.bfloat16)
    vmem = pl.BlockSpec(memory_space=pltpu.VMEM)
    return pl.pallas_call(
        truncate_kernel,
        out_shape=(square, square),
        in_specs=[pl.BlockSpec(memory_space=pltpu.SMEM), vmem, vmem],
        out_specs=(vmem, vmem),
        scratch_shapes=[
            pltpu.VMEM((width, rank), jnp.bfloat16),
            pltpu.VMEM((rank, width), jnp.bfloat16),
            pltpu.VMEM((rank, width), jnp.bfloat16),
            pltpu.VMEM((rank, rank), jnp.float32),
            pltpu.VMEM((rank, rank), jnp.float32),
        ],
        compiler_params=pltpu.CompilerParams(vmem_limit_bytes=24 * 2**20),
        cost_estimate=pl.CostEstimate(flops=2 * width**3 * 3, bytes_accessed=3 * width**2, transcendentals=0),
    )(table, ground, cols)


def per_device(psi_start, left_site, left_terms, right_terms, start_cols, sector_table):
    ground = lanczos(
        sector_table, psi_start[0, 0], left_site[0, 0], left_terms[0, 0], right_terms[0, 0],
        lax.axis_size("sec"),
    )
    kept, dens = truncate(sector_table, ground, start_cols[0])
    segs = lax.axis_size("seg")
    back = lax.ppermute(dens, "seg", [(i + 1, i) for i in range(segs - 1)])
    return (kept[None, None], back[None, None])


def solution(mesh):
    placed = (
        P("seg", "sec", None, None),
        P("seg", "sec", None, None),
        P("seg", "sec", None, None, None),
        P("seg", "sec", None, None, None),
        P("sec", None, None),
        P("sec", None),
    )
    return jax.shard_map(
        per_device,
        mesh=mesh,
        in_specs=placed,
        out_specs=(P("seg", "sec", None, None), P("seg", "sec", None, None)),
        check_vma=False,
    )
```

time: 195 us -> 181 us (0.928)
  the two profiles are of different devices: /device:TPU:24 before, /device:TPU:1 now
where the time goes in v3:
time: 181 us; the launch traced here: 179 us
  Pallas kernels  150 us (83%)
  waiting for transfers between devices  23.1 us (13%)
  starting transfers between devices  3.07 us (2%)
  local copies, waits for them, and re-layouts  1.84 us (1%)
    pallas_call x1, Pallas kernels, lanczos(): pl.pallas_call(lanczos_kernel, out_shape=jax.ShapeDtypeStruct(square, jnp...  139 us
    ppermute x1, waiting for transfers between devices, per_device(): back = lax.ppermute(dens, 'seg', [(i + 1, i) for i in range(segs - 1)])  23.1 us
    pallas_call x1, Pallas kernels, truncate(): pl.pallas_call(truncate_kernel, out_shape=(square, square), in_specs=[pl....  11.7 us
  transfers between devices with their start and end apart: 1, of which 1 were waited for; matrix products, arithmetic and copies ran while one was open for 0% of the time, Pallas kernels for 0%

profile of v3, /device:TPU:1, one launch (start us, length us, event | category | flops | bytes accessed | tf_op | source)
XLA Modules:
  0.0 179.2 jit_solution(7208303571005932165)
XLA Ops:
  0.6 0.0 copy-start
  0.6 0.0 copy-start.1
  0.7 138.7 %shard_map.77.ground_ref = bf16[512,512]{1,0:T(8,128)(2,1)} custom-call(s32[1,3]{1,0:T(1,128)} %table_ref.3, bf16[512,512]{1,0:T(8,128)(2,1)} %bitcast.11, bf16[512,512]{1,0:T(8,128)(2,1)} %bitcast.12, bf16[3,512,512]{2,1,0:T(8,128)(2,1)} %bitcast.9, bf16[2,512,512]{2,1,0:T(8,128)(2,1)} %bitcast.10), custom_call_target="tpu_custom_call" | custom-call | flops 4294967296 | bytes 2097152 | tf_op jit(solution)/shard_map/pallas_call | solution.py:352
  139.4 0.0 copy-done
  139.4 0.0 copy-done.1
  139.4 0.0 copy-start.2
  139.4 1.0 copy-done.2
  140.5 11.7 %shard_map.78 = (bf16[512,512]{1,0:T(8,128)(2,1)}, bf16[512,512]{1,0:T(8,128)(2,1)S(1)}) custom-call(s32[1,3]{1,0:T(1,128)S(1)} %copy-done.1, bf16[512,512]{1,0:T(8,128)(2,1)S(1)} %copy-done.2, bf16[512,256]{1,0:T(8,128)(2,1)S(1)} %bitcast.7), custom_call_target="tpu_custom_call" | custom-call | flops 805306368 | bytes 786432 | tf_op jit(solution)/shard_map/pallas_call | solution.py:472
  152.2 3.1 %collective-permute-start = (bf16[512,512]{1,0:T(8,128)(2,1)S(1)}, bf16[512,512]{1,0:T(8,128)(2,1)S(1)}, u32[]{:S(2)}, u32[]{:S(2)}) collective-permute-start(bf16[512,512]{1,0:T(8,128)(2,1)S(1)} %get-tuple-element.5), channel_id=1, source_target_pairs={{8,0},{16,8},{24,16},{32,24},{40,32},{48,40},{56,48},{64,56},{72,6... | collective-permute-start | bytes 1572872 | tf_op jit(solution)/shard_map/ppermute | solution.py:496
  155.3 23.1 %collective-permute-done = bf16[512,512]{1,0:T(8,128)(2,1)S(1)} collective-permute-done((bf16[512,512]{1,0:T(8,128)(2,1)S(1)}, bf16[512,512]{1,0:T(8,128)(2,1)S(1)}, u32[]{:S(2)}, u32[]{:S(2)}) %collective-permute-start) | collective-permute-done | bytes 524320 | tf_op jit(solution)/shard_map/ppermute | solution.py:496
  178.4 0.8 copy.9
Async XLA Ops:
  0.6 138.8 %copy-start = (bf16[1,512,256]{2,1,0:T(8,128)(2,1)S(1)}, bf16[1,512,256]{2,1,0:T(8,128)(2,1)}, u32[]{:S(2)}) copy-start(bf16[1,512,256]{2,1,0:T(8,128)(2,1)} %param.10) | copy-start | bytes 786436
  0.6 138.8 %copy-start.1 = (s32[1,3]{1,0:T(1,128)S(1)}, s32[1,3]{1,0:T(1,128)}, u32[]{:S(2)}) copy-start(s32[1,3]{1,0:T(1,128)} %table_ref.3) | copy-start | bytes 40
  139.4 1.0 copy-start.2
  152.2 26.2 %collective-permute-start = (bf16[512,512]{1,0:T(8,128)(2,1)S(1)}, bf16[512,512]{1,0:T(8,128)(2,1)S(1)}, u32[]{:S(2)}, u32[]{:S(2)}) collective-permute-start(bf16[512,512]{1,0:T(8,128)(2,1)S(1)} %get-tuple-element.5), channel_id=1, source_target_pairs={{8,0},{16,8},{24,16},{32,24},{40,32},{48,40},{56,48},{64,56},{72,6... | collective-permute-start | bytes 1572872 | tf_op jit(solution)/shard_map/ppermute | solution.py:496

commit v4 on v3

--- a/solution.py
+++ b/solution.py
@@ -10,8 +10,8 @@
 eps = 1e-06
 MESH = pl.DeviceIdType.MESH
 CHUNKS = 8
-ENV_AT = 4
-AHEAD = 1
+ENV_AT = 1
+LEG = 4
 
 
 def dot(left, right):
@@ -46,9 +46,9 @@
     table_ref, psi_hbm, site_hbm, terms_hbm, right_hbm, ground_ref,
     psi, site, terms, right,
     start, start_z, start_x, site_t, part, built, env, vec, vec_z,
-    low_z, low_x, image, resid, resid_z, ritz, adj, pull, pull_out, pull_in,
-    sums1, sums2, sums3,
-    load, z_send, z_recv, x_send, x_recv, env_send, env_recv, pull_send, pull_recv, sum_send, sum_recv,
+    held, low_z, low_x, image, resid, resid_z, adj, pull, pull_out, pull_in,
+    sums1, sums2, deltas,
+    load, a_send, a_recv, z_send, z_recv, x_send, x_recv, env_send, env_recv, pull_send, pull_recv, sum_send, sum_recv,
 ):
     seg, sec = lax.axis_index("seg"), lax.axis_index("sec")
     segs, secs = lax.axis_size("seg"), lax.axis_size("sec")
@@ -60,10 +60,16 @@
     relay = lax.rem(sec + 2 - 4 * parity + secs, secs)
     source = lax.rem(sec - 2 + 4 * parity + secs, secs)
     nxt, prv = lax.rem(seg + 1, segs), lax.rem(seg + segs - 1, segs)
+    core, z_lo, line = lax.rem(seg, 2), lax.rem(lax.div(seg, 2), 8), lax.div(seg, 16)
+
+    def along_z(distance):
+        place = lax.rem(parity * 8 + z_lo + distance, 16)
+        return ((line * 8 + lax.rem(place, 8)) * 2 + core, sec - parity + lax.div(place, 8))
+
     peers = [(seg, lax.rem(sec + d, secs)) for d in range(1, secs)]
 
     barrier = pltpu.get_barrier_semaphore()
-    neighbours = peers + [(nxt, sec), (prv, sec)]
+    neighbours = peers + [(nxt, sec), (prv, sec), along_z(LEG), along_z(16 - LEG)]
     for device in neighbours:
         pl.semaphore_signal(barrier, inc=1, device_id=device, device_id_type=MESH)
 
@@ -82,12 +88,25 @@
     def halves(b):
         return pl.ds(pl.multiple_of(b * half, half), half)
 
-    def z_copy(phase, i, held, target):
+    def leg(i):
+        return along_z(LEG + lax.rem(i, 2) * (16 - 2 * LEG))
+
+    def a_copy(phase, i, block):
         return pltpu.make_async_remote_copy(
-            held.at[chunk(i)], target.at[chunk(i)],
-            z_send.at[phase, i], z_recv.at[phase, i],
+            block.at[chunk(i)], (start_z, resid_z)[phase].at[chunk(i)],
+            a_send.at[phase, i], a_recv.at[phase, i],
             device_id=(seg, partner), device_id_type=MESH,
         )
+
+    def z_copy(phase, i, target):
+        return a_copy(phase, i, (start, resid)[phase])
+
+    def forward(phase, i, block, target):
+        return
+
+    def forward_two(phase, j, block, target):
+        forward(phase, 2 * j, block, target)
+        forward(phase, 2 * j + 1, block, target)
 
     def x_copy(i):
         return pltpu.make_async_remote_copy(
@@ -102,9 +121,9 @@
             device_id=(nxt, sec), device_id_type=MESH,
         )
 
-    def pull_copy():
+    def pull_copy(k):
         return pltpu.make_async_remote_copy(
-            pull_out, pull_in, pull_send.at[0], pull_recv.at[0],
+            pull_out.at[k], pull_in.at[k], pull_send.at[k], pull_recv.at[k],
             device_id=(seg, source), device_id_type=MESH,
         )
 
@@ -139,7 +158,7 @@
     zero = jnp.zeros((1, 1), jnp.float32)
     blank = jnp.zeros((8, 128), jnp.float32)
     sums1[sec] = blank
-    sums3[sec] = blank
+    sums2[sec] = blank
     loads[0].wait()
 
     def begin(i, norm):
@@ -155,7 +174,7 @@
     share(0, sums1)
 
     def send_start(i, _):
-        z_copy(0, i, start, start_z).start()
+        a_copy(0, i, start).start()
         return 0
 
     lax.fori_loop(0, CHUNKS, send_start, 0)
@@ -181,6 +200,7 @@
     lax.fori_loop(0, 3, build, 0)
 
     loads[3].wait()
+    forward_two(0, 0, start, start_z)
     collect(0, sums1)
     scale = 1.0 / jnp.sqrt(summed(sums1)[:, 0:1] + eps)
     has_env = jnp.where(seg > 0, 1.0, 0.0).astype(jnp.float32)
@@ -199,7 +219,7 @@
     env_z, env_x = env.at[2 - parity], env.at[1 + parity]
 
     def first_z(i):
-        z_copy(0, i, start, start_z).wait_recv()
+        z_copy(0, i, start_z).wait_recv()
         x_copy(i).start()
         piece = scaled(i, start_z)
         vec_z[chunk(i)] = piece
@@ -209,137 +229,198 @@
         x_copy(i).wait_recv()
         low_x[chunk(i)] = (dot(scaled(i, start_x), right_x[...]) * has_x).astype(jnp.bfloat16)
 
-    def arrive(i, _):
-        first_z(i)
-        first_x(i - 1)
-        return 0
-
-    def arrive_send(i, _):
-        env_copy(i - ENV_AT).start()
-        return arrive(i, 0)
-
-    first_z(0)
-    lax.fori_loop(1, ENV_AT, arrive, 0)
-    lax.fori_loop(ENV_AT, CHUNKS, arrive_send, 0)
+    pairs = CHUNKS // 2
+
+    def arrive(j, _):
+        forward_two(0, j, start, start_z)
+        first_z(2 * j - 2)
+        first_z(2 * j - 1)
+
+        @pl.when(j > 1)
+        def _():
+            first_x(2 * j - 4)
+            first_x(2 * j - 3)
+
+        return 0
 
     def send_env(i, _):
         env_copy(i).start()
         return 0
 
-    lax.fori_loop(CHUNKS - ENV_AT, CHUNKS, send_env, 0)
-    first_x(CHUNKS - 1)
-
-    def apply(i, _):
+    def arrive_send(j, _):
+        send_env(2 * (j - ENV_AT), 0)
+        send_env(2 * (j - ENV_AT) + 1, 0)
+        return arrive(j, 0)
+
+    lax.fori_loop(1, ENV_AT, arrive, 0)
+    lax.fori_loop(ENV_AT, pairs, arrive_send, 0)
+    lax.fori_loop(2 * (pairs - ENV_AT), CHUNKS, send_env, 0)
+    first_z(CHUNKS - 2)
+    first_z(CHUNKS - 1)
+    for i in range(CHUNKS - 4, CHUNKS):
+        first_x(i)
+
+    def image_of(i):
         env_copy(i).wait_recv()
         value = dot(env[0, chunk(i)], vec[...])
         value += dot(env_z[chunk(i)], low_z[...])
         value += dot(env_x[chunk(i)], low_x[...])
-        value = jnp.where(mask(i * rows, rows), value * has_env, 0.0)
+        return jnp.where(mask(i * rows, rows), value * has_env, 0.0)
+
+    def emit(i, value, guess, sums):
         mine = vec[chunk(i)].astype(jnp.float32)
-        along, size = total(mine * value), total(mine * mine)
-        ratio = jnp.where(size > 0.0, along / jnp.where(size > 0.0, size, 1.0), 0.0)
-        piece = value - ratio * mine
+        piece = value - guess * mine
         image[chunk(i)] = piece
         resid[chunk(i)] = piece.astype(jnp.bfloat16)
-        sums2[sec, pl.ds(i, 1)] = pack([along, size, total(piece * piece), total(mine * piece), ratio])
-        return 0
-
-    def send_resid(i, _):
-        z_copy(1, i, resid, resid_z).start()
-        return 0
-
-    def apply_send(i, _):
-        apply(i, 0)
-        return send_resid(i, 0)
-
-    lax.fori_loop(0, AHEAD, apply_send, 0)
-    lax.fori_loop(AHEAD, CHUNKS, apply, 0)
+        a_copy(1, i, resid).start()
+        return sums[0] + total(mine * value), sums[1] + total(mine * mine)
+
+    def quotient(along, size):
+        return jnp.where(size > 0.0, along / jnp.where(size > 0.0, size, 1.0), 0.0)
+
+    value = image_of(0)
+    mine = vec[chunk(0)].astype(jnp.float32)
+    guess = quotient(total(mine * value), total(mine * mine))
+    sums = emit(0, value, guess, (zero, zero))
+
+    def apply(i, sums):
+        return emit(i, image_of(i), guess, sums)
+
+    sums = lax.fori_loop(1, CHUNKS // 2, apply, sums)
+    forward_two(1, 0, resid, resid_z)
+    along, size = lax.fori_loop(CHUNKS // 2, CHUNKS, apply, sums)
+
+    def turned(matrix, vector):
+        for b in range(2):
+            block = slice(b * half, (b + 1) * half)
+            adj[block] = dot_left_t(matrix[:, block], vector[...]).astype(jnp.bfloat16)
+
+    def pull_away(k, vector):
+        turned(env_x, vector)
+
+        def piece(b, _):
+            pull_out[k, halves(b)] = (dot_right_t(adj[halves(b)], right_x[...]) * has_x).astype(jnp.bfloat16)
+            return 0
+
+        lax.fori_loop(0, 2, piece, 0)
+        pull_copy(k).start()
+
+    def pull_here(k, vector):
+        turned(env_z, vector)
+
+        def piece(b, _):
+            pull[k, halves(b)] = dot_right_t(adj[halves(b)], right_z[...])
+            return 0
+
+        lax.fori_loop(0, 2, piece, 0)
+
+    pull_away(0, resid)
+    pull_away(1, vec)
+    forward_two(1, 1, resid, resid_z)
+    pull_here(0, resid)
+    pull_here(1, vec)
+
+    def diagonal(b, sums):
+        image_r = dot(env[0, halves(b)], resid[...])
+        image_v = dot(env[0, halves(b)], vec[...])
+        mine_r, mine_v = resid[halves(b)].astype(jnp.float32), vec[halves(b)].astype(jnp.float32)
+        return (
+            sums[0] + total(mine_r * image_r),
+            sums[1] + total(mine_r * image_v + mine_v * image_r),
+            sums[2] + total(mine_v * image_v),
+        )
+
+    square_r, mixed, square_v = lax.fori_loop(0, 2, diagonal, (zero, zero, zero))
+    ratio = quotient(along, size)
+
+    def norms(i, sums):
+        mine = vec[chunk(i)].astype(jnp.float32)
+        piece = image[chunk(i)] + (guess - ratio) * mine
+        return sums[0] + total(piece * piece), sums[1] + total(mine * piece)
+
+    rho, cross = lax.fori_loop(0, CHUNKS, norms, (zero, zero))
+    pull_copy(0).wait_recv()
+    pull_copy(1).wait_recv()
+
+    def join(i, sums):
+        both = pull[0, chunk(i)] + pull_in[0, chunk(i)].astype(jnp.float32)
+        pull[0, chunk(i)] = both
+        base = vec_z[chunk(i)].astype(jnp.float32)
+        return (
+            sums[0] + total(both * base),
+            sums[1] + total(pull[1, chunk(i)] * base),
+            sums[2] + total(pull_in[1, chunk(i)].astype(jnp.float32) * base),
+        )
+
+    base_r, base_v, base_x = lax.fori_loop(0, CHUNKS, join, (zero, zero, zero))
+
+    def meet(i, sums):
+        z_copy(1, i, resid_z).wait_recv()
+        other = resid_z[chunk(i)].astype(jnp.float32)
+        terms = (pull[0, chunk(i)], pull[1, chunk(i)], pull_in[1, chunk(i)].astype(jnp.float32))
+        return tuple(old + jnp.sum(term * other, axis=0, keepdims=True) for old, term in zip(sums, terms))
+
+    def meet_two(j, sums):
+        forward_two(1, j, resid, resid_z)
+        return meet(2 * j - 3, meet(2 * j - 4, sums))
+
+    line_sums = (jnp.zeros((1, width), jnp.float32),) * 3
+    line_sums = lax.fori_loop(2, pairs, meet_two, line_sums)
+    line_sums = lax.fori_loop(CHUNKS - 4, CHUNKS, meet, line_sums)
+    met_r, met_v, met_x = [jnp.sum(line, axis=1, keepdims=True) for line in line_sums]
+    sums2[sec, pl.ds(0, 1)] = pack(
+        [along, size, rho, cross, ratio, guess]
+        + [
+            term * has_env
+            for term in (square_r + met_r, mixed + met_v, square_v, met_x, base_r, base_v, base_x)
+        ]
+    )
     share(1, sums2)
-    lax.fori_loop(AHEAD, CHUNKS, send_resid, 0)
     collect(1, sums2)
 
-    totals = summed(sums2)
-    alpha, size = totals[:, 0:1], totals[:, 1:2]
-    beta_sq = zero
-    for s in range(secs):
-        tile = sums2[s]
-        delta = tile[:, 4:5] - alpha
-        beta_sq = beta_sq + total(tile[:, 2:3] + 2.0 * delta * tile[:, 3:4] + delta * delta * tile[:, 1:2])
-    beta = jnp.sqrt(jnp.maximum(beta_sq, 0.0) + eps)
+    gathered = jnp.sum(sums2[...], axis=1)
+    column = lambda k: gathered[:, k : k + 1]
+    over = lambda value: jnp.sum(value, axis=0, keepdims=True)
+    alpha, size = over(column(0)), over(column(1))
+    delta = column(4) - alpha
+    resid_sq = jnp.maximum(over(column(2) + delta * (2.0 * column(3) + delta * column(1))), 0.0)
+    overlap = over(column(3) + delta * column(1))
+    beta_sq = resid_sq + eps
+    beta = jnp.sqrt(beta_sq)
     inverse = 1.0 / beta
-
-    def shift(s, i):
-        return sums2[s, pl.ds(i, 1)][:, 4:5] - alpha
-
-    def second(i, sums):
+    own = column(5) - alpha
+    deltas[...] = jnp.broadcast_to(own, deltas.shape)
+    picked = lambda order: jnp.concatenate([deltas[s : s + 1] for s in order], axis=0)[:, 0:1]
+    beside = picked([s + 1 - 2 * (s % 2) for s in range(secs)])
+    across = picked([(s + 2 - 4 * (s % 2)) % secs for s in range(secs)])
+    gamma = over(
+        column(6) + own * (column(7) + own * column(8)) + across * column(9)
+        + beside * (column(10) + own * column(11) + across * column(12))
+    ) / beta_sq
+    lowest = 0.5 * (alpha + gamma) - jnp.sqrt(0.25 * (alpha - gamma) ** 2 + beta_sq)
+    first = gamma - lowest
+    united_sq = first * first * size - 2.0 * first * overlap + resid_sq
+    factor = math.sqrt(secs * width * width) / jnp.sqrt(jnp.maximum(united_sq, 0.0) + eps)
+    back = deltas[pl.ds(sec, 1)][:, 0:1]
+
+    def finish(i, _):
         mine = vec[chunk(i)].astype(jnp.float32)
-        piece = ((image[chunk(i)] + shift(sec, i) * mine) * inverse).astype(jnp.bfloat16)
-        ritz[chunk(i)] = piece
-        wide = piece.astype(jnp.float32)
-        return sums[0] + total(mine * wide), sums[1] + total(wide * wide)
-
-    overlap, size2 = lax.fori_loop(0, CHUNKS, second, (zero, zero))
-
-    for b in range(2):
-        adj[b * half : (b + 1) * half] = dot_left_t(env_x[:, b * half : (b + 1) * half], ritz[...]).astype(jnp.bfloat16)
-
-    def pull_x(b, _):
-        pull_out[halves(b)] = (dot_right_t(adj[halves(b)], right_x[...]) * has_x).astype(jnp.bfloat16)
-        return 0
-
-    lax.fori_loop(0, 2, pull_x, 0)
-    pull_copy().start()
-    for b in range(2):
-        adj[b * half : (b + 1) * half] = dot_left_t(env_z[:, b * half : (b + 1) * half], ritz[...]).astype(jnp.bfloat16)
-
-    def pull_z(b, gamma):
-        pull[halves(b)] = dot_right_t(adj[halves(b)], right_z[...])
-        return gamma + total(ritz[halves(b)].astype(jnp.float32) * dot(env[0, halves(b)], ritz[...]))
-
-    gamma = lax.fori_loop(0, 2, pull_z, zero)
-    pull_copy().wait_recv()
-
-    def join(i, partial):
-        both = pull[chunk(i)] + pull_in[chunk(i)].astype(jnp.float32)
-        pull[chunk(i)] = both
-        return partial + shift(partner, i) * total(both * vec_z[chunk(i)].astype(jnp.float32))
-
-    cross = lax.fori_loop(0, CHUNKS, join, zero)
-
-    def meet(i, partial):
-        z_copy(1, i, resid, resid_z).wait_recv()
-        return partial + total(pull[chunk(i)] * resid_z[chunk(i)].astype(jnp.float32))
-
-    cross = lax.fori_loop(0, CHUNKS, meet, cross)
-    gamma = (gamma + cross * inverse) * has_env
-    sums3[sec, pl.ds(0, 1)] = pack([gamma, overlap, size2])
-    share(2, sums3)
-    collect(2, sums3)
-    totals = summed(sums3)
-    gamma = totals[:, 0:1]
-    lowest = 0.5 * (alpha + gamma) - jnp.sqrt(0.25 * (alpha - gamma) ** 2 + beta * beta)
-    first = gamma - lowest
-    united_sq = (
-        first * first * size - 2.0 * first * beta * totals[:, 1:2] + beta * beta * totals[:, 2:3]
-    )
-    factor = math.sqrt(secs * width * width) / jnp.sqrt(jnp.maximum(united_sq, 0.0) + eps)
-
-    def finish(i, _):
-        united = first * vec[chunk(i)].astype(jnp.float32) - beta * ritz[chunk(i)].astype(jnp.float32)
-        ground_ref[chunk(i)] = (united * factor).astype(jnp.bfloat16)
+        ritz = ((image[chunk(i)] + back * mine) * inverse).astype(jnp.bfloat16).astype(jnp.float32)
+        ground_ref[chunk(i)] = ((first * mine - beta * ritz) * factor).astype(jnp.bfloat16)
         return 0
 
     lax.fori_loop(0, CHUNKS, finish, 0)
 
     def drain(i, _):
-        z_copy(0, i, start, start_z).wait_send()
-        z_copy(1, i, resid, resid_z).wait_send()
+        a_copy(0, i, start).wait_send()
+        a_copy(1, i, resid).wait_send()
         x_copy(i).wait_send()
         env_copy(i).wait_send()
         return 0
 
     lax.fori_loop(0, CHUNKS, drain, 0)
-    pull_copy().wait_send()
+    pull_copy(0).wait_send()
+    pull_copy(1).wait_send()
 
 
 def lanczos(table, psi, site, terms, right, secs):
@@ -357,10 +438,11 @@
         scratch_shapes=[
             blocks(), blocks(), blocks(3), blocks(2),
             blocks(), blocks(), blocks(), blocks(), blocks(), blocks(3), blocks(3), blocks(), blocks(),
-            blocks(), blocks(), wide, blocks(), blocks(), blocks(), blocks(), wide, blocks(), blocks(),
-            sums, sums, sums,
-            dma((4,)), dma((2, CHUNKS)), dma((2, CHUNKS)), dma((CHUNKS,)), dma((CHUNKS,)),
-            dma((CHUNKS,)), dma((CHUNKS,)), dma((1,)), dma((1,)), dma((3, secs)), dma((3, secs)),
+            blocks(2), blocks(), blocks(), wide, blocks(), blocks(), blocks(),
+            pltpu.VMEM((2, *square), jnp.float32), blocks(2), blocks(2),
+            sums, sums, pltpu.VMEM((secs, 128), jnp.float32),
+            dma((4,)), dma((2, CHUNKS)), dma((2, CHUNKS)), dma((2, CHUNKS)), dma((2, CHUNKS)), dma((CHUNKS,)), dma((CHUNKS,)),
+            dma((CHUNKS,)), dma((CHUNKS,)), dma((2,)), dma((2,)), dma((2, secs)), dma((2, secs)),
         ],
         compiler_params=pltpu.CompilerParams(
             collective_id=1, has_side_effects=True, vmem_limit_bytes=62 * 2**20

time: 181 us -> 170 us (0.939)
  waiting for transfers between devices: 23.1 us -> 11.1 us
  Pallas kernels: 150 us -> 154 us
    ppermute x1, waiting for transfers between devices: 23.1 us -> 11.1 us  [per_device(): back = lax.ppermute(dens, 'seg', [(i + 1, i) for i in range(segs - 1)])]
    pallas_call x1, Pallas kernels: 139 us -> 143 us  [lanczos(): pl.pallas_call(lanczos_kernel, out_shape=jax.ShapeDtypeStruct(square, jnp...]
where the time goes in v4:
time: 170 us
  Pallas kernels  154 us (91%)
  waiting for transfers between devices  11.1 us (7%)
  starting transfers between devices  1.91 us (1%)
  local copies, waits for them, and re-layouts  1.84 us (1%)
    pallas_call x1, Pallas kernels, lanczos(): pl.pallas_call(lanczos_kernel, out_shape=jax.ShapeDtypeStruct(square, jnp...  143 us
    pallas_call x1, Pallas kernels, truncate(): pl.pallas_call(truncate_kernel, out_shape=(square, square), in_specs=[pl....  11.7 us
    ppermute x1, waiting for transfers between devices, per_device(): back = lax.ppermute(dens, 'seg', [(i + 1, i) for i in range(segs - 1)])  11.1 us
  transfers between devices with their start and end apart: 1, of which 1 were waited for; matrix products, arithmetic and copies ran while one was open for 0% of the time, Pallas kernels for 0%

profile of v4, /device:TPU:1, one launch (start us, length us, event | category | flops | bytes accessed | tf_op | source)
XLA Modules:
  0.0 169.9 jit_solution(6955720597015129069)
XLA Ops:
  0.6 0.0 copy-start
  0.6 0.0 copy-start.1
  0.7 142.7 %shard_map.77.ground_ref = bf16[512,512]{1,0:T(8,128)(2,1)} custom-call(s32[1,3]{1,0:T(1,128)} %table_ref.3, bf16[512,512]{1,0:T(8,128)(2,1)} %bitcast.11, bf16[512,512]{1,0:T(8,128)(2,1)} %bitcast.12, bf16[3,512,512]{2,1,0:T(8,128)(2,1)} %bitcast.9, bf16[2,512,512]{2,1,0:T(8,128)(2,1)} %bitcast.10), custom_call_target="tpu_custom_call" | custom-call | flops 4294967296 | bytes 2097152 | tf_op jit(solution)/shard_map/pallas_call | solution.py:433
  143.3 0.0 copy-done
  143.3 0.0 copy-done.1
  143.3 0.0 copy-start.2
  143.3 1.0 copy-done.2
  144.4 11.7 %shard_map.78 = (bf16[512,512]{1,0:T(8,128)(2,1)}, bf16[512,512]{1,0:T(8,128)(2,1)S(1)}) custom-call(s32[1,3]{1,0:T(1,128)S(1)} %copy-done.1, bf16[512,512]{1,0:T(8,128)(2,1)S(1)} %copy-done.2, bf16[512,256]{1,0:T(8,128)(2,1)S(1)} %bitcast.7), custom_call_target="tpu_custom_call" | custom-call | flops 805306368 | bytes 786432 | tf_op jit(solution)/shard_map/pallas_call | solution.py:554
  156.1 1.9 %collective-permute-start = (bf16[512,512]{1,0:T(8,128)(2,1)S(1)}, bf16[512,512]{1,0:T(8,128)(2,1)S(1)}, u32[]{:S(2)}, u32[]{:S(2)}) collective-permute-start(bf16[512,512]{1,0:T(8,128)(2,1)S(1)} %get-tuple-element.5), channel_id=1, source_target_pairs={{8,0},{16,8},{24,16},{32,24},{40,32},{48,40},{56,48},{64,56},{72,6... | collective-permute-start | bytes 1572872 | tf_op jit(solution)/shard_map/ppermute | solution.py:578
  158.0 11.1 %collective-permute-done = bf16[512,512]{1,0:T(8,128)(2,1)S(1)} collective-permute-done((bf16[512,512]{1,0:T(8,128)(2,1)S(1)}, bf16[512,512]{1,0:T(8,128)(2,1)S(1)}, u32[]{:S(2)}, u32[]{:S(2)}) %collective-permute-start) | collective-permute-done | bytes 524320 | tf_op jit(solution)/shard_map/ppermute | solution.py:578
  169.1 0.8 copy.9
Async XLA Ops:
  0.6 142.7 %copy-start = (bf16[1,512,256]{2,1,0:T(8,128)(2,1)S(1)}, bf16[1,512,256]{2,1,0:T(8,128)(2,1)}, u32[]{:S(2)}) copy-start(bf16[1,512,256]{2,1,0:T(8,128)(2,1)} %param.10) | copy-start | bytes 786436
  0.6 142.7 %copy-start.1 = (s32[1,3]{1,0:T(1,128)S(1)}, s32[1,3]{1,0:T(1,128)}, u32[]{:S(2)}) copy-start(s32[1,3]{1,0:T(1,128)} %table_ref.3) | copy-start | bytes 40
  143.3 1.0 copy-start.2
  156.1 13.0 %collective-permute-start = (bf16[512,512]{1,0:T(8,128)(2,1)S(1)}, bf16[512,512]{1,0:T(8,128)(2,1)S(1)}, u32[]{:S(2)}, u32[]{:S(2)}) collective-permute-start(bf16[512,512]{1,0:T(8,128)(2,1)S(1)} %get-tuple-element.5), channel_id=1, source_target_pairs={{8,0},{16,8},{24,16},{32,24},{40,32},{48,40},{56,48},{64,56},{72,6... | collective-permute-start | bytes 1572872 | tf_op jit(solution)/shard_map/ppermute | solution.py:578

commit v5 on v4

--- a/solution.py
+++ b/solution.py
@@ -42,13 +42,65 @@
     return row
 
 
-def lanczos_kernel(
-    table_ref, psi_hbm, site_hbm, terms_hbm, right_hbm, ground_ref,
-    psi, site, terms, right,
+def fdot(left, right):
+    return jnp.dot(left, right, precision=lax.Precision.HIGHEST, preferred_element_type=jnp.float32)
+
+
+def invert_factor(block, panel):
+    size = block.shape[0]
+    lane = lax.broadcasted_iota(jnp.int32, (1, size), 1)
+    sub = lax.broadcasted_iota(jnp.int32, (8, size), 0)
+    done = []
+    rest = block
+    for j in range(0, size, panel):
+        drop = j % 8
+        cols = [jnp.broadcast_to(rest[:, j + c : j + c + 1], rest.shape) for c in range(panel)]
+        row = lax.broadcasted_iota(jnp.int32, rest.shape, 0)
+        inside = (lane >= j) & (lane < j + panel)
+        rest = jnp.where(inside, jnp.where(lane - j == row - drop, 1.0, 0.0), rest)
+        scales = jnp.ones((8, size), jnp.float32)
+        for c in range(panel):
+            at = drop + c
+            pivot = cols[c][at : at + 1]
+            inverse = pl.reciprocal(pivot, approx=True)
+            inverse = inverse * (2.0 - pivot * inverse)
+            scales = jnp.where(sub == at, lax.rsqrt(pivot), scales)
+            factor = jnp.where(row > at, cols[c] * inverse, 0.0)
+            for d in range(c + 1, panel):
+                cols[d] = cols[d] - factor * cols[d][at : at + 1]
+            rest = rest - factor * rest[at : at + 1]
+        done.append(rest[:8] * scales)
+        rest = rest[8:]
+    full = jnp.concatenate(done, axis=0)
+    r = lax.broadcasted_iota(jnp.int32, (size, size), 0)
+    q = lax.broadcasted_iota(jnp.int32, (size, size), 1)
+    return jnp.where(r >= q, full, 0.0)
+
+
+def split_dot(left, right):
+    result = None
+    rest = left
+    for _ in range(3):
+        part = rest.astype(jnp.bfloat16)
+        rest = rest - part.astype(jnp.float32)
+        term = dot(part, right)
+        result = term if result is None else result + term
+    return result
+
+
+def rebuilt(turned, state):
+    coeff = dot(turned, state).astype(jnp.bfloat16)
+    return dot(turned.T, coeff)
+
+
+def update_kernel(
+    table_ref, psi_hbm, site_hbm, terms_hbm, right_hbm, cols_hbm, kept_ref, dens_ref,
+    psi, site, terms, right, cols,
     start, start_z, start_x, site_t, part, built, env, vec, vec_z,
     held, low_z, low_x, image, resid, resid_z, adj, pull, pull_out, pull_in,
     sums1, sums2, deltas,
-    load, a_send, a_recv, z_send, z_recv, x_send, x_recv, env_send, env_recv, pull_send, pull_recv, sum_send, sum_recv,
+    ground, ground_n, basis_t, basis_n, range_t, gram, part_n,
+    load, a_send, a_recv, z_send, z_recv, x_send, x_recv, env_send, env_recv, pull_send, pull_recv, sum_send, sum_recv, back_send, back_recv,
 ):
     seg, sec = lax.axis_index("seg"), lax.axis_index("sec")
     segs, secs = lax.axis_size("seg"), lax.axis_size("sec")
@@ -78,6 +130,7 @@
         pltpu.make_async_copy(site_hbm, site, load.at[1]),
         pltpu.make_async_copy(terms_hbm, terms, load.at[2]),
         pltpu.make_async_copy(right_hbm, right, load.at[3]),
+        pltpu.make_async_copy(cols_hbm, cols, load.at[4]),
     ]
     for copy in loads:
         copy.start()
@@ -125,6 +178,11 @@
         return pltpu.make_async_remote_copy(
             pull_out.at[k], pull_in.at[k], pull_send.at[k], pull_recv.at[k],
             device_id=(seg, source), device_id_type=MESH,
+        )
+
+    def back_copy(k, block, target):
+        return pltpu.make_async_remote_copy(
+            block, target, back_send.at[k], back_recv.at[k], device_id=(prv, sec), device_id_type=MESH
         )
 
     def sum_copies(phase, buffer):
@@ -406,7 +464,7 @@
     def finish(i, _):
         mine = vec[chunk(i)].astype(jnp.float32)
         ritz = ((image[chunk(i)] + back * mine) * inverse).astype(jnp.bfloat16).astype(jnp.float32)
-        ground_ref[chunk(i)] = ((first * mine - beta * ritz) * factor).astype(jnp.bfloat16)
+        ground[chunk(i)] = ((first * mine - beta * ritz) * factor).astype(jnp.bfloat16)
         return 0
 
     lax.fori_loop(0, CHUNKS, finish, 0)
@@ -422,160 +480,89 @@
     pull_copy(0).wait_send()
     pull_copy(1).wait_send()
 
-
-def lanczos(table, psi, site, terms, right, secs):
+    rank = cols.shape[1]
+    near = rank // 2
+    low, high = slice(0, near), slice(near, rank)
+    ground_back = back_copy(0, ground, ground_n)
+    ground_back.start()
+    loads[4].wait()
+    kept_rank = table_ref[0, 2]
+    keep = jnp.where(lax.broadcasted_iota(jnp.int32, (1, rank), 1) < kept_rank, 1.0, 0.0)
+    row = lax.broadcasted_iota(jnp.int32, (rank, rank), 0)
+    col = lax.broadcasted_iota(jnp.int32, (rank, rank), 1)
+    gram[...] = jnp.where((row == col) & (col >= kept_rank), 1.0, 0.0)
+    for b in range(2):
+        block = slice(b * half, (b + 1) * half)
+        ranged = (dot(ground[block], cols[...]) * keep).astype(jnp.bfloat16)
+        turned_range = ranged.T
+        range_t[:, block] = turned_range
+        gram[...] += dot(turned_range, ranged)
+    leading = invert_factor(gram[low, low], 8)
+    basis_t[low] = split_dot(leading, range_t[low]).astype(jnp.bfloat16)
+    backs = [back_copy(1 + b, basis_t.at[block], basis_n.at[block]) for b, block in enumerate((low, high))]
+    backs[0].start()
+    upper = fdot(leading, gram[low, high])
+    upper_t = upper.T
+    trailing = invert_factor(gram[high, high] - fdot(upper_t, upper), 8)
+    corner = -fdot(trailing, fdot(upper_t, leading))
+    basis_t[high] = (split_dot(corner, range_t[low]) + split_dot(trailing, range_t[high])).astype(jnp.bfloat16)
+    backs[1].start()
+
+    kept_ref[...] = rebuilt(basis_t[...], ground[...]).astype(jnp.bfloat16)
+
+    ground_back.wait_recv()
+    backs[0].wait_recv()
+    part_n[...] = rebuilt(basis_n[low], ground_n[...])
+    backs[1].wait_recv()
+    start[...] = (part_n[...] + rebuilt(basis_n[high], ground_n[...])).astype(jnp.bfloat16)
+    has_next = jnp.where(seg < segs - 1, 1.0 / width, 0.0).astype(jnp.float32)
+
+    def density(b, _):
+        dens_ref[halves(b)] = (dot_right_t(start[halves(b)], start[...]) * has_next).astype(jnp.bfloat16)
+        return 0
+
+    lax.fori_loop(0, 2, density, 0)
+    ground_back.wait_send()
+    for copy in backs:
+        copy.wait_send()
+
+
+def update(table, psi, site, terms, right, cols, secs):
     width = psi.shape[0]
+    rank = cols.shape[1]
     square = (width, width)
+    tall = pltpu.VMEM((rank, width), jnp.bfloat16)
     blocks = lambda *lead: pltpu.VMEM((*lead, *square), jnp.bfloat16)
     wide = pltpu.VMEM(square, jnp.float32)
     sums = pltpu.VMEM((secs, 8, 128), jnp.float32)
     dma = pltpu.SemaphoreType.DMA
     return pl.pallas_call(
-        lanczos_kernel,
-        out_shape=jax.ShapeDtypeStruct(square, jnp.bfloat16),
-        in_specs=[pl.BlockSpec(memory_space=pltpu.SMEM)] + [pl.BlockSpec(memory_space=pl.ANY)] * 4,
-        out_specs=pl.BlockSpec(memory_space=pltpu.VMEM),
+        update_kernel,
+        out_shape=(jax.ShapeDtypeStruct(square, jnp.bfloat16),) * 2,
+        in_specs=[pl.BlockSpec(memory_space=pltpu.SMEM)] + [pl.BlockSpec(memory_space=pl.ANY)] * 5,
+        out_specs=(pl.BlockSpec(memory_space=pltpu.VMEM),) * 2,
         scratch_shapes=[
-            blocks(), blocks(), blocks(3), blocks(2),
+            blocks(), blocks(), blocks(3), blocks(2), pltpu.VMEM((width, rank), jnp.bfloat16),
             blocks(), blocks(), blocks(), blocks(), blocks(), blocks(3), blocks(3), blocks(), blocks(),
             blocks(2), blocks(), blocks(), wide, blocks(), blocks(), blocks(),
             pltpu.VMEM((2, *square), jnp.float32), blocks(2), blocks(2),
             sums, sums, pltpu.VMEM((secs, 128), jnp.float32),
-            dma((4,)), dma((2, CHUNKS)), dma((2, CHUNKS)), dma((2, CHUNKS)), dma((2, CHUNKS)), dma((CHUNKS,)), dma((CHUNKS,)),
-            dma((CHUNKS,)), dma((CHUNKS,)), dma((2,)), dma((2,)), dma((2, secs)), dma((2, secs)),
+            blocks(), blocks(), tall, tall, tall, pltpu.VMEM((rank, rank), jnp.float32), wide,
+            dma((5,)), dma((2, CHUNKS)), dma((2, CHUNKS)), dma((2, CHUNKS)), dma((2, CHUNKS)), dma((CHUNKS,)), dma((CHUNKS,)),
+            dma((CHUNKS,)), dma((CHUNKS,)), dma((2,)), dma((2,)), dma((2, secs)), dma((2, secs)), dma((3,)), dma((3,)),
         ],
         compiler_params=pltpu.CompilerParams(
             collective_id=1, has_side_effects=True, vmem_limit_bytes=62 * 2**20
         ),
         cost_estimate=pl.CostEstimate(flops=16 * 2 * width**3, bytes_accessed=8 * width**2, transcendentals=0),
-    )(table, psi, site, terms, right)
-
-
-def fdot(left, right):
-    return jnp.dot(left, right, precision=lax.Precision.HIGHEST, preferred_element_type=jnp.float32)
-
-
-def spread_lane(tile, lane):
-    return jnp.broadcast_to(tile[:, lane : lane + 1], tile.shape)
-
-
-def spread_row(tile, row):
-    return jnp.broadcast_to(tile[row : row + 1, :], tile.shape)
-
-
-def invert_factor(block, panel):
-    size = block.shape[0]
-    count = size // 8
-    tiles = [block[8 * t : 8 * t + 8] for t in range(count)]
-    lane = lax.broadcasted_iota(jnp.int32, (8, size), 1)
-    sub = lax.broadcasted_iota(jnp.int32, (8, size), 0)
-    scales = [None] * count
-    for j in range(0, size, panel):
-        top, base = j // 8, j % 8
-        cols = [
-            {t: spread_lane(tiles[t], j + c) for t in range(top, count)} for c in range(panel)
-        ]
-        inside = (lane >= j) & (lane < j + panel)
-        for t in range(top, count):
-            tiles[t] = jnp.where(inside, jnp.where((lane - j == sub + 8 * t - j) , 1.0, 0.0) if t == top else 0.0, tiles[t])
-        for c in range(panel):
-            row = base + c
-            pivot = spread_row(cols[c][top], row)
-            inverse = 1.0 / pivot
-            scale = lax.rsqrt(pivot)
-            scales[top] = scale if scales[top] is None else jnp.where(sub >= row, scale, scales[top])
-            below = sub > row
-            factor = {}
-            for t in range(top, count):
-                f = cols[c][t] * inverse
-                factor[t] = jnp.where(below, f, 0.0) if t == top else f
-            for d in range(c + 1, panel):
-                head = spread_row(cols[d][top], row)
-                for t in range(top, count):
-                    cols[d][t] = cols[d][t] - factor[t] * head
-            line = spread_row(tiles[top], row)
-            for t in range(top, count):
-                tiles[t] = tiles[t] - factor[t] * line
-    out = [tiles[t] * scales[t] for t in range(count)]
-    full = jnp.concatenate(out, axis=0)
-    r = lax.broadcasted_iota(jnp.int32, (size, size), 0)
-    q = lax.broadcasted_iota(jnp.int32, (size, size), 1)
-    return jnp.where(r >= q, full, 0.0)
-
-
-def split_dot(left, right):
-    result = None
-    rest = left
-    for _ in range(3):
-        part = rest.astype(jnp.bfloat16)
-        rest = rest - part.astype(jnp.float32)
-        term = dot(part, right)
-        result = term if result is None else result + term
-    return result
-
-
-def truncate_kernel(table_ref, ground_ref, cols_ref, kept_ref, dens_ref, basis, basis_t, range_t, gram, inv):
-    width, rank = cols_ref.shape
-    half = rank // 2
-    lane = lax.broadcasted_iota(jnp.int32, (1, rank), 1)
-    keep = jnp.where(lane < table_ref[0, 2], 1.0, 0.0)
-    for b in range(2):
-        block = pl.ds(b * 256, 256)
-        rng = (dot(ground_ref[block], cols_ref[...]) * keep).astype(jnp.bfloat16)
-        basis[block] = rng
-        range_t[:, block] = rng.T
-    row = lax.broadcasted_iota(jnp.int32, (rank, rank), 0)
-    col = lax.broadcasted_iota(jnp.int32, (rank, rank), 1)
-    gram[...] = dot(range_t[...], basis[...]) + jnp.where((row == col) & (col >= table_ref[0, 2]), 1.0, 0.0)
-    first = invert_factor(gram[:half, :half], 8)
-    upper = fdot(first, gram[:half, half:])
-    upper_t = upper.T
-    second = invert_factor(gram[half:, half:] - fdot(upper_t, upper), 8)
-    inv[:half, :half] = first
-    inv[:half, half:] = jnp.zeros((half, half), jnp.float32)
-    inv[half:, :half] = -fdot(second, fdot(upper_t, first))
-    inv[half:, half:] = second
-    basis_t[...] = split_dot(inv[...], range_t[...]).astype(jnp.bfloat16)
-    basis[...] = basis_t[...].T
-    coeff = dot(basis_t[...], ground_ref[...]).astype(jnp.bfloat16)
-    for b in range(2):
-        block = pl.ds(b * 256, 256)
-        kept_ref[block] = dot(basis[block], coeff).astype(jnp.bfloat16)
-    kept_t = kept_ref[...].T
-    for b in range(2):
-        block = pl.ds(b * 256, 256)
-        dens_ref[block] = (dot(kept_ref[block], kept_t) * (1.0 / width)).astype(jnp.bfloat16)
-
-
-def truncate(table, ground, cols):
-    width, rank = cols.shape
-    square = jax.ShapeDtypeStruct((width, width), jnp.bfloat16)
-    vmem = pl.BlockSpec(memory_space=pltpu.VMEM)
-    return pl.pallas_call(
-        truncate_kernel,
-        out_shape=(square, square),
-        in_specs=[pl.BlockSpec(memory_space=pltpu.SMEM), vmem, vmem],
-        out_specs=(vmem, vmem),
-        scratch_shapes=[
-            pltpu.VMEM((width, rank), jnp.bfloat16),
-            pltpu.VMEM((rank, width), jnp.bfloat16),
-            pltpu.VMEM((rank, width), jnp.bfloat16),
-            pltpu.VMEM((rank, rank), jnp.float32),
-            pltpu.VMEM((rank, rank), jnp.float32),
-        ],
-        compiler_params=pltpu.CompilerParams(vmem_limit_bytes=24 * 2**20),
-        cost_estimate=pl.CostEstimate(flops=2 * width**3 * 3, bytes_accessed=3 * width**2, transcendentals=0),
-    )(table, ground, cols)
+    )(table, psi, site, terms, right, cols)
 
 
 def per_device(psi_start, left_site, left_terms, right_terms, start_cols, sector_table):
-    ground = lanczos(
+    kept, back = update(
         sector_table, psi_start[0, 0], left_site[0, 0], left_terms[0, 0], right_terms[0, 0],
-        lax.axis_size("sec"),
+        start_cols[0], lax.axis_size("sec"),
     )
-    kept, dens = truncate(sector_table, ground, start_cols[0])
-    segs = lax.axis_size("seg")
-    back = lax.ppermute(dens, "seg", [(i + 1, i) for i in range(segs - 1)])
     return (kept[None, None], back[None, None])
 
 

time: 170 us -> 167 us (0.982)
  waiting for transfers between devices: 11.1 us -> 0 us
  Pallas kernels: 154 us -> 163 us
  starting transfers between devices: 1.91 us -> 0 us
  local copies, waits for them, and re-layouts: 1.84 us -> 3.74 us
    ppermute x1 -> x0, waiting for transfers between devices: 11.1 us -> none  [per_device(): back = lax.ppermute(dens, 'seg', [(i + 1, i) for i in range(segs - 1)])]
    pallas_call x2 -> x1, Pallas kernels: 154 us -> 163 us  [update(): pl.pallas_call(update_kernel, out_shape=(jax.ShapeDtypeStruct(square, jnp...]
    ppermute x1 -> x0, starting transfers between devices: 1.91 us -> none  [per_device(): back = lax.ppermute(dens, 'seg', [(i + 1, i) for i in range(segs - 1)])]
    unnamed x7 -> x2, local copies, waits for them, and re-layouts: 1.84 us -> 3.74 us
  transfers between devices with their start and end apart: 1 -> 0, of which waited for: 1 -> 0; matrix products, arithmetic and copies ran while one was open for 0% -> 0% of each run, Pallas kernels for 0% -> 0%
where the time goes in v5:
time: 167 us
  Pallas kernels  163 us (98%)
  local copies, waits for them, and re-layouts  3.74 us (2%)
    pallas_call x1, Pallas kernels, update(): pl.pallas_call(update_kernel, out_shape=(jax.ShapeDtypeStruct(square, jnp...  163 us
    unnamed x2, local copies, waits for them, and re-layouts  3.74 us

profile of v5, /device:TPU:1, one launch (start us, length us, event | category | flops | bytes accessed | tf_op | source)
XLA Modules:
  0.0 166.9 jit_solution(17591571985580721558)
XLA Ops:
  0.6 162.5 %shard_map.77 = (bf16[512,512]{1,0:T(8,128)(2,1)}, bf16[512,512]{1,0:T(8,128)(2,1)}) custom-call(s32[1,3]{1,0:T(1,128)} %table_ref.1, bf16[512,512]{1,0:T(8,128)(2,1)} %bitcast.11, bf16[512,512]{1,0:T(8,128)(2,1)} %bitcast.12, bf16[3,512,512]{2,1,0:T(8,128)(2,1)} %bitcast.9, bf16[2,512,512]{2,1,0:T(8,128)(2,1)} %bitcast.10, bf16[512,256]{1,0:T(8,128)(2,1)} %bitcast.13), custom_call_target="tpu_custom_call" | custom-call | flops 4294967296 | bytes 2097152 | tf_op jit(solution)/shard_map/pallas_call | solution.py:539
  163.2 1.9 %copy.10 = bf16[1,1,512,512]{3,2,1,0:T(8,128)(2,1)} copy(bf16[1,1,512,512]{3,2,1,0:T(8,128)(2,1)} %bitcast.8) | data formatting | bytes 1048576
  165.1 1.9 %copy.11 = bf16[1,1,512,512]{3,2,1,0:T(8,128)(2,1)} copy(bf16[1,1,512,512]{3,2,1,0:T(8,128)(2,1)} %bitcast.7) | data formatting | bytes 1048576

commit v6 on v5

--- a/solution.py
+++ b/solution.py
@@ -11,7 +11,6 @@
 MESH = pl.DeviceIdType.MESH
 CHUNKS = 8
 ENV_AT = 1
-LEG = 4
 
 
 def dot(left, right):
@@ -97,10 +96,10 @@
     table_ref, psi_hbm, site_hbm, terms_hbm, right_hbm, cols_hbm, kept_ref, dens_ref,
     psi, site, terms, right, cols,
     start, start_z, start_x, site_t, part, built, env, vec, vec_z,
-    held, low_z, low_x, image, resid, resid_z, adj, pull, pull_out, pull_in,
+    low_z, low_x, image, resid, resid_z, adj, pull, pull_out, pull_in,
     sums1, sums2, deltas,
     ground, ground_n, basis_t, basis_n, range_t, gram, part_n,
-    load, a_send, a_recv, z_send, z_recv, x_send, x_recv, env_send, env_recv, pull_send, pull_recv, sum_send, sum_recv, back_send, back_recv,
+    load, z_send, z_recv, x_send, x_recv, env_send, env_recv, pull_send, pull_recv, sum_send, sum_recv, back_send, back_recv,
 ):
     seg, sec = lax.axis_index("seg"), lax.axis_index("sec")
     segs, secs = lax.axis_size("seg"), lax.axis_size("sec")
@@ -112,16 +111,10 @@
     relay = lax.rem(sec + 2 - 4 * parity + secs, secs)
     source = lax.rem(sec - 2 + 4 * parity + secs, secs)
     nxt, prv = lax.rem(seg + 1, segs), lax.rem(seg + segs - 1, segs)
-    core, z_lo, line = lax.rem(seg, 2), lax.rem(lax.div(seg, 2), 8), lax.div(seg, 16)
-
-    def along_z(distance):
-        place = lax.rem(parity * 8 + z_lo + distance, 16)
-        return ((line * 8 + lax.rem(place, 8)) * 2 + core, sec - parity + lax.div(place, 8))
-
     peers = [(seg, lax.rem(sec + d, secs)) for d in range(1, secs)]
 
     barrier = pltpu.get_barrier_semaphore()
-    neighbours = peers + [(nxt, sec), (prv, sec), along_z(LEG), along_z(16 - LEG)]
+    neighbours = peers + [(nxt, sec), (prv, sec)]
     for device in neighbours:
         pl.semaphore_signal(barrier, inc=1, device_id=device, device_id_type=MESH)
 
@@ -141,25 +134,13 @@
     def halves(b):
         return pl.ds(pl.multiple_of(b * half, half), half)
 
-    def leg(i):
-        return along_z(LEG + lax.rem(i, 2) * (16 - 2 * LEG))
-
-    def a_copy(phase, i, block):
+    def z_copy(phase, i):
+        block, target = ((start, start_z), (resid, resid_z))[phase]
         return pltpu.make_async_remote_copy(
-            block.at[chunk(i)], (start_z, resid_z)[phase].at[chunk(i)],
-            a_send.at[phase, i], a_recv.at[phase, i],
+            block.at[chunk(i)], target.at[chunk(i)],
+            z_send.at[phase, i], z_recv.at[phase, i],
             device_id=(seg, partner), device_id_type=MESH,
         )
-
-    def z_copy(phase, i, target):
-        return a_copy(phase, i, (start, resid)[phase])
-
-    def forward(phase, i, block, target):
-        return
-
-    def forward_two(phase, j, block, target):
-        forward(phase, 2 * j, block, target)
-        forward(phase, 2 * j + 1, block, target)
 
     def x_copy(i):
         return pltpu.make_async_remote_copy(
@@ -188,7 +169,7 @@
     def sum_copies(phase, buffer):
         return [
             pltpu.make_async_remote_copy(
-                buffer.at[sec], buffer.at[sec],
+                buffer.at[pl.ds(sec, 1)], buffer.at[pl.ds(sec, 1)],
                 sum_send.at[phase, d], sum_recv.at[phase, d],
                 device_id=peers[d], device_id_type=MESH,
             )
@@ -204,7 +185,7 @@
             copy.wait()
 
     def summed(buffer):
-        return jnp.sum(jnp.sum(buffer[...], axis=0), axis=0, keepdims=True)
+        return jnp.sum(buffer[...], axis=0, keepdims=True)
 
     live_rows, live_cols = table_ref[0, 0], table_ref[0, 1]
 
@@ -214,9 +195,6 @@
         return (i < live_rows) & (j < live_cols)
 
     zero = jnp.zeros((1, 1), jnp.float32)
-    blank = jnp.zeros((8, 128), jnp.float32)
-    sums1[sec] = blank
-    sums2[sec] = blank
     loads[0].wait()
 
     def begin(i, norm):
@@ -224,18 +202,18 @@
         start[chunk(i)] = piece.astype(jnp.bfloat16)
         return norm + total(piece * piece)
 
-    norm = lax.fori_loop(0, CHUNKS, begin, zero)
-    sums1[sec, pl.ds(0, 1)] = pack([norm])
-
+    norm = begin(0, zero)
     pl.semaphore_wait(barrier, len(neighbours))
-
+    z_copy(0, 0).start()
+    norm = lax.fori_loop(1, CHUNKS, begin, norm)
+    sums1[pl.ds(sec, 1)] = pack([norm])
     share(0, sums1)
 
     def send_start(i, _):
-        a_copy(0, i, start).start()
-        return 0
-
-    lax.fori_loop(0, CHUNKS, send_start, 0)
+        z_copy(0, i).start()
+        return 0
+
+    lax.fori_loop(1, CHUNKS, send_start, 0)
 
     loads[1].wait()
     site_t[...] = site[...].T
@@ -258,7 +236,6 @@
     lax.fori_loop(0, 3, build, 0)
 
     loads[3].wait()
-    forward_two(0, 0, start, start_z)
     collect(0, sums1)
     scale = 1.0 / jnp.sqrt(summed(sums1)[:, 0:1] + eps)
     has_env = jnp.where(seg > 0, 1.0, 0.0).astype(jnp.float32)
@@ -277,7 +254,7 @@
     env_z, env_x = env.at[2 - parity], env.at[1 + parity]
 
     def first_z(i):
-        z_copy(0, i, start_z).wait_recv()
+        z_copy(0, i).wait_recv()
         x_copy(i).start()
         piece = scaled(i, start_z)
         vec_z[chunk(i)] = piece
@@ -290,7 +267,6 @@
     pairs = CHUNKS // 2
 
     def arrive(j, _):
-        forward_two(0, j, start, start_z)
         first_z(2 * j - 2)
         first_z(2 * j - 1)
 
@@ -330,7 +306,7 @@
         piece = value - guess * mine
         image[chunk(i)] = piece
         resid[chunk(i)] = piece.astype(jnp.bfloat16)
-        a_copy(1, i, resid).start()
+        z_copy(1, i).start()
         return sums[0] + total(mine * value), sums[1] + total(mine * mine)
 
     def quotient(along, size):
@@ -344,9 +320,7 @@
     def apply(i, sums):
         return emit(i, image_of(i), guess, sums)
 
-    sums = lax.fori_loop(1, CHUNKS // 2, apply, sums)
-    forward_two(1, 0, resid, resid_z)
-    along, size = lax.fori_loop(CHUNKS // 2, CHUNKS, apply, sums)
+    along, size = lax.fori_loop(1, CHUNKS, apply, sums)
 
     def turned(matrix, vector):
         for b in range(2):
@@ -374,7 +348,6 @@
 
     pull_away(0, resid)
     pull_away(1, vec)
-    forward_two(1, 1, resid, resid_z)
     pull_here(0, resid)
     pull_here(1, vec)
 
@@ -413,20 +386,14 @@
     base_r, base_v, base_x = lax.fori_loop(0, CHUNKS, join, (zero, zero, zero))
 
     def meet(i, sums):
-        z_copy(1, i, resid_z).wait_recv()
+        z_copy(1, i).wait_recv()
         other = resid_z[chunk(i)].astype(jnp.float32)
         terms = (pull[0, chunk(i)], pull[1, chunk(i)], pull_in[1, chunk(i)].astype(jnp.float32))
         return tuple(old + jnp.sum(term * other, axis=0, keepdims=True) for old, term in zip(sums, terms))
 
-    def meet_two(j, sums):
-        forward_two(1, j, resid, resid_z)
-        return meet(2 * j - 3, meet(2 * j - 4, sums))
-
-    line_sums = (jnp.zeros((1, width), jnp.float32),) * 3
-    line_sums = lax.fori_loop(2, pairs, meet_two, line_sums)
-    line_sums = lax.fori_loop(CHUNKS - 4, CHUNKS, meet, line_sums)
+    line_sums = lax.fori_loop(0, CHUNKS, meet, (jnp.zeros((1, width), jnp.float32),) * 3)
     met_r, met_v, met_x = [jnp.sum(line, axis=1, keepdims=True) for line in line_sums]
-    sums2[sec, pl.ds(0, 1)] = pack(
+    sums2[pl.ds(sec, 1)] = pack(
         [along, size, rho, cross, ratio, guess]
         + [
             term * has_env
@@ -436,7 +403,7 @@
     share(1, sums2)
     collect(1, sums2)
 
-    gathered = jnp.sum(sums2[...], axis=1)
+    gathered = sums2[...]
     column = lambda k: gathered[:, k : k + 1]
     over = lambda value: jnp.sum(value, axis=0, keepdims=True)
     alpha, size = over(column(0)), over(column(1))
@@ -470,8 +437,8 @@
     lax.fori_loop(0, CHUNKS, finish, 0)
 
     def drain(i, _):
-        a_copy(0, i, start).wait_send()
-        a_copy(1, i, resid).wait_send()
+        z_copy(0, i).wait_send()
+        z_copy(1, i).wait_send()
         x_copy(i).wait_send()
         env_copy(i).wait_send()
         return 0
@@ -534,7 +501,7 @@
     tall = pltpu.VMEM((rank, width), jnp.bfloat16)
     blocks = lambda *lead: pltpu.VMEM((*lead, *square), jnp.bfloat16)
     wide = pltpu.VMEM(square, jnp.float32)
-    sums = pltpu.VMEM((secs, 8, 128), jnp.float32)
+    sums = pltpu.VMEM((secs, 128), jnp.float32)
     dma = pltpu.SemaphoreType.DMA
     return pl.pallas_call(
         update_kernel,
@@ -544,11 +511,11 @@
         scratch_shapes=[
             blocks(), blocks(), blocks(3), blocks(2), pltpu.VMEM((width, rank), jnp.bfloat16),
             blocks(), blocks(), blocks(), blocks(), blocks(), blocks(3), blocks(3), blocks(), blocks(),
-            blocks(2), blocks(), blocks(), wide, blocks(), blocks(), blocks(),
+            blocks(), blocks(), wide, blocks(), blocks(), blocks(),
             pltpu.VMEM((2, *square), jnp.float32), blocks(2), blocks(2),
             sums, sums, pltpu.VMEM((secs, 128), jnp.float32),
             blocks(), blocks(), tall, tall, tall, pltpu.VMEM((rank, rank), jnp.float32), wide,
-            dma((5,)), dma((2, CHUNKS)), dma((2, CHUNKS)), dma((2, CHUNKS)), dma((2, CHUNKS)), dma((CHUNKS,)), dma((CHUNKS,)),
+            dma((5,)), dma((2, CHUNKS)), dma((2, CHUNKS)), dma((CHUNKS,)), dma((CHUNKS,)),
             dma((CHUNKS,)), dma((CHUNKS,)), dma((2,)), dma((2,)), dma((2, secs)), dma((2, secs)), dma((3,)), dma((3,)),
         ],
         compiler_params=pltpu.CompilerParams(

time: 167 us -> 164 us (0.982)
  Pallas kernels: 163 us -> 160 us
    pallas_call x1, Pallas kernels: 163 us -> 160 us  [update(): pl.pallas_call(update_kernel, out_shape=(jax.ShapeDtypeStruct(square, jnp...]
where the time goes in v6:
time: 164 us
  Pallas kernels  160 us (98%)
  local copies, waits for them, and re-layouts  3.74 us (2%)
    pallas_call x1, Pallas kernels, update(): pl.pallas_call(update_kernel, out_shape=(jax.ShapeDtypeStruct(square, jnp...  160 us
    unnamed x2, local copies, waits for them, and re-layouts  3.74 us

profile of v6, /device:TPU:1, one launch (start us, length us, event | category | flops | bytes accessed | tf_op | source)
XLA Modules:
  0.0 163.9 jit_solution(10653899720108875623)
XLA Ops:
  0.6 159.5 %shard_map.77 = (bf16[512,512]{1,0:T(8,128)(2,1)}, bf16[512,512]{1,0:T(8,128)(2,1)}) custom-call(s32[1,3]{1,0:T(1,128)} %table_ref.1, bf16[512,512]{1,0:T(8,128)(2,1)} %bitcast.11, bf16[512,512]{1,0:T(8,128)(2,1)} %bitcast.12, bf16[3,512,512]{2,1,0:T(8,128)(2,1)} %bitcast.9, bf16[2,512,512]{2,1,0:T(8,128)(2,1)} %bitcast.10, bf16[512,256]{1,0:T(8,128)(2,1)} %bitcast.13), custom_call_target="tpu_custom_call" | custom-call | flops 4294967296 | bytes 2097152 | tf_op jit(solution)/shard_map/pallas_call | solution.py:506
  160.2 1.9 %copy.10 = bf16[1,1,512,512]{3,2,1,0:T(8,128)(2,1)} copy(bf16[1,1,512,512]{3,2,1,0:T(8,128)(2,1)} %bitcast.8) | data formatting | bytes 1048576
  162.0 1.9 %copy.11 = bf16[1,1,512,512]{3,2,1,0:T(8,128)(2,1)} copy(bf16[1,1,512,512]{3,2,1,0:T(8,128)(2,1)} %bitcast.7) | data formatting | bytes 1048576

commit v7 on v6

--- a/solution.py
+++ b/solution.py
@@ -93,7 +93,7 @@
 
 
 def update_kernel(
-    table_ref, psi_hbm, site_hbm, terms_hbm, right_hbm, cols_hbm, kept_ref, dens_ref,
+    table_ref, psi_hbm, site_hbm, terms_hbm, right_hbm, cols_hbm, kept_ref, next_ref,
     psi, site, terms, right, cols,
     start, start_z, start_x, site_t, part, built, env, vec, vec_z,
     low_z, low_x, image, resid, resid_z, adj, pull, pull_out, pull_in,
@@ -481,14 +481,7 @@
     backs[0].wait_recv()
     part_n[...] = rebuilt(basis_n[low], ground_n[...])
     backs[1].wait_recv()
-    start[...] = (part_n[...] + rebuilt(basis_n[high], ground_n[...])).astype(jnp.bfloat16)
-    has_next = jnp.where(seg < segs - 1, 1.0 / width, 0.0).astype(jnp.float32)
-
-    def density(b, _):
-        dens_ref[halves(b)] = (dot_right_t(start[halves(b)], start[...]) * has_next).astype(jnp.bfloat16)
-        return 0
-
-    lax.fori_loop(0, 2, density, 0)
+    next_ref[...] = (part_n[...] + rebuilt(basis_n[high], ground_n[...])).astype(jnp.bfloat16)
     ground_back.wait_send()
     for copy in backs:
         copy.wait_send()
@@ -525,11 +518,34 @@
     )(table, psi, site, terms, right, cols)
 
 
+def finish_kernel(kept_ref, next_ref, out_ref, dens_ref):
+    width = next_ref.shape[0]
+    out_ref[...] = kept_ref[...]
+    has_next = lax.axis_index("seg") < lax.axis_size("seg") - 1
+    scale = jnp.where(has_next, 1.0 / width, 0.0).astype(jnp.float32)
+    for b in range(2):
+        block = slice(b * (width // 2), (b + 1) * (width // 2))
+        dens_ref[block] = (dot_right_t(next_ref[block], next_ref[...]) * scale).astype(jnp.bfloat16)
+
+
+def finish(kept, kept_next):
+    square = jax.ShapeDtypeStruct(kept.shape, jnp.bfloat16)
+    vmem = pl.BlockSpec(memory_space=pltpu.VMEM)
+    return pl.pallas_call(
+        finish_kernel,
+        out_shape=(square, square),
+        in_specs=[vmem, vmem],
+        out_specs=(vmem, vmem),
+        compiler_params=pltpu.CompilerParams(vmem_limit_bytes=62 * 2**20),
+    )(kept, kept_next)
+
+
 def per_device(psi_start, left_site, left_terms, right_terms, start_cols, sector_table):
-    kept, back = update(
+    kept, kept_next = update(
         sector_table, psi_start[0, 0], left_site[0, 0], left_terms[0, 0], right_terms[0, 0],
         start_cols[0], lax.axis_size("sec"),
     )
+    kept, back = finish(kept, kept_next)
     return (kept[None, None], back[None, None])
 
 

time: 164 us -> 162 us (0.988)
  local copies, waits for them, and re-layouts: 3.74 us -> 0 us
    unnamed x2 -> x0, local copies, waits for them, and re-layouts: 3.74 us -> none
    pallas_call x0 -> x1, Pallas kernels: none -> 2.59 us  [finish(): pl.pallas_call(finish_kernel, out_shape=(square, square), in_specs=[vmem,...]
where the time goes in v7:
time: 162 us
  Pallas kernels  161 us (99%)
    pallas_call x1, Pallas kernels, update(): pl.pallas_call(update_kernel, out_shape=(jax.ShapeDtypeStruct(square, jnp...  159 us

profile of v7, /device:TPU:1, one launch (start us, length us, event | category | flops | bytes accessed | tf_op | source)
XLA Modules:
  0.0 162.1 jit_solution(5905738893257107483)
XLA Ops:
  0.6 158.8 %shard_map.77 = (bf16[512,512]{1,0:T(8,128)(2,1)}, bf16[512,512]{1,0:T(8,128)(2,1)}) custom-call(s32[1,3]{1,0:T(1,128)} %table_ref.1, bf16[512,512]{1,0:T(8,128)(2,1)} %bitcast.9, bf16[512,512]{1,0:T(8,128)(2,1)} %bitcast.10, bf16[3,512,512]{2,1,0:T(8,128)(2,1)} %bitcast.7, bf16[2,512,512]{2,1,0:T(8,128)(2,1)} %bitcast.8, bf16[512,256]{1,0:T(8,128)(2,1)} %bitcast.13), custom_call_target="tpu_custom_call" | custom-call | flops 4294967296 | bytes 2097152 | tf_op jit(solution)/shard_map/pallas_call | solution.py:499
  159.5 2.6 %shard_map.78 = (bf16[512,512]{1,0:T(8,128)(2,1)}, bf16[512,512]{1,0:T(8,128)(2,1)}) custom-call(bf16[512,512]{1,0:T(8,128)(2,1)} %get-tuple-element.6.kept_ref, bf16[512,512]{1,0:T(8,128)(2,1)} %get-tuple-element.7.next_ref), custom_call_target="tpu_custom_call" | custom-call | tf_op jit(solution)/shard_map/pallas_call | solution.py:534
